TPU v7x, 256 devices: a whole 4x4x8 slice. The times are simulated.
256 devices in a mesh: gx: 64 (over z_lo, y, x, core), row: 4 (over z_hi).
Axes of the slice: x: 4, y: 4, z: 8 (z_hi: 4, z_lo: 2; z = z_hi * 2 + z_lo), core: 2. Of those that a mesh axis runs over, the one named last changes fastest.
Arguments:
- amplitudes: float32 [1024, 4096], P('gx', 'row'), may hold values from -6 to 6
- integrals: float32 [4096, 131072], P('row', 'gx'), may hold values from -0.1875 to 0.1875
- cd_irrep: int32 [32], P('row'), may hold values from 0 to 7
- ab_irrep: int32 [1024], P('gx'), may hold values from 0 to 7
- allowed: int32 [8, 8], replicated, may hold values 0 or 1
- pair_occ: int32 [1024, 2], P(('gx', 'row')), may hold values from 0 to 99
- occ_energy: float32 [100], replicated, may hold values from -1 to -0.25
- ab_energy: float32 [131072], replicated, may hold values from 1 to 4
Outputs:
- residual: float32 [1024, 131072], P(('gx', 'row'))
- update: float32 [1024, 131072], P(('gx', 'row'))
All inputs are finite; a program needn't handle non-finite values.
Results may differ from a plain program's by a relative error of at most 0.000071.
Values sent between devices are 32-bit elements; how exact they have to be, the bound alone decides.
No kernel may reach another device: no remote copies, remote signals or barrier semaphores. Data moves between devices by JAX's collectives and lax.ppermute only.
A program may use at most 128 MiB of HBM per device.

v0:
```python
import jax
import jax.numpy as jnp
from jax import lax
from jax.sharding import PartitionSpec as P

BLK = 128


def body(amplitudes, integrals, cd_irrep, ab_irrep, allowed, pair_occ, occ_energy, ab_energy):
    irrep_labels = jnp.arange(allowed.shape[0], dtype=jnp.int32)
    cd_onehot = (cd_irrep[:, None] == irrep_labels[None, :]).astype(jnp.float32)
    ab_onehot = (ab_irrep[:, None] == irrep_labels[None, :]).astype(jnp.float32)
    irrep_table = allowed.astype(jnp.float32)
    block_mask = jnp.dot(
        jnp.dot(cd_onehot, irrep_table, precision=lax.Precision.HIGHEST),
        ab_onehot.T,
        precision=lax.Precision.HIGHEST,
    )
    cd_rows, ab_cols = integrals.shape
    effective = (
        integrals.reshape(cd_rows // BLK, BLK, ab_cols // BLK, BLK) * block_mask[:, None, :, None]
    ).reshape(cd_rows, ab_cols)
    partial_value = jnp.dot(
        lax.all_gather(amplitudes, "gx", axis=0, tiled=True),
        effective,
        precision=lax.Precision.HIGHEST,
        preferred_element_type=jnp.float32,
    )
    arrived = lax.all_to_all(partial_value, "gx", split_axis=0, concat_axis=1, tiled=True)
    residual = lax.psum_scatter(arrived, "row", scatter_dimension=0, tiled=True)
    occ_labels = jnp.arange(occ_energy.shape[0], dtype=jnp.int32)
    pair_onehot = (pair_occ[:, :, None] == occ_labels[None, None, :]).astype(jnp.float32)
    pair_energy = jnp.sum(pair_onehot * occ_energy[None, None, :], axis=(1, 2))
    update = residual / (ab_energy[None, :] - pair_energy[:, None])
    return (residual, update)


def solution(mesh):
    return jax.shard_map(
        body,
        mesh=mesh,
        in_specs=(
            P("gx", "row"),
            P("row", "gx"),
            P("row"),
            P("gx"),
            P(),
            P(("gx", "row"), None),
            P(),
            P(),
        ),
        out_specs=(P(("gx", "row"), None), P(("gx", "row"), None)),
        check_vma=False,
    )
```

profile of v0, /device:TPU:1, one launch (start us, length us, event | category | flops | bytes accessed | tf_op | source)
XLA Modules:
  0.0 575.8 jit_solution(4756469213630064393)
XLA Ops:
  7.2 0.0 all-gather.2.cloned.1.call-start
  7.2 0.7 all-gather.2.cloned.1.call-update
  7.9 0.0 all-reduce.3.cloned.1.call-start
  7.9 0.9 fusion.4
  8.8 0.8 fusion.2
  9.7 112.9 %all-gather.2.cloned.1.call-done = f32[1024,1024]{1,0:T(8,128)} async-done(((f32[16,1024]{1,0:T(8,128)}), f32[1024,1024]{1,0:T(8,128)}) %all-gather.2.cloned.1.call-update) | async-done | bytes 4194320 | tf_op jit(solution)/shard_map/all_gather | solution.py:24
  122.5 0.0 copy-start
  122.5 0.6 mul.19
  123.2 2.8 copy-done
  125.9 34.0 %fusion = f32[2048,1024]{0,1:T(8,128)S(1)} fusion(f32[1024,1024]{1,0:T(8,128)} %all-gather.2.cloned.1.call-done, f32[1024,2048]{1,0:T(8,128)S(1)} %copy-done, f32[128,8,16,128]{3,2,1,0:T(8,128)S(1)} %bitcast.14), kind=kOutput, calls=%fused_computation.1 | convolution fusion | flops 25771900928 | bytes 29360128 | tf_op jit(solution)/shard_map/dot_general | solution.py:23
  159.9 101.4 %all_to_all.19 = f32[64,16,2048]{2,1,0:T(8,128)S(1)} all-to-all(f32[64,16,2048]{2,1,0:T(8,128)S(1)} %bitcast.15), channel_id=1, replica_groups=mesh['gx'=64,'row'=4] {'gx'}, dimensions={0} | all-to-all | bytes 16777216 | tf_op jit(solution)/shard_map/all_to_all | solution.py:29
  261.4 3.8 copy.15
  265.2 0.0 copy-start.4
  265.2 0.0 copy-start.2
  265.2 0.0 copy-start.3
  265.2 0.0 all-reduce.3.cloned.1.call-update
  265.2 0.6 copy-done.4
  265.9 0.6 dynamic-slice
  267.1 0.0 copy-done.2
  267.1 0.0 copy-done.3
  267.1 0.2 select_reduce_fusion
  267.3 296.6 %all-reduce.3.cloned.1.call-done = f32[16,131072]{1,0:T(8,128)} async-done(((f32[16,131072]{1,0:T(8,128)}), f32[16,131072]{1,0:T(8,128)}) %all-reduce.3.cloned.1.call-update) | async-done | bytes 8388624
  563.9 0.0 copy-done.1
  563.9 5.0 subtract_divide_fusion
  (1 shorter events, 0.0 us)
Async XLA Ops:
  7.2 115.4 %all-gather.2.cloned.1.call-start = ((), (), s32[]{:S(2)}) async-start(), calls=%async_computation.1 | async-start | bytes 4259840 | tf_op jit(solution)/shard_map/all_gather | solution.py:24
  7.9 556.0 %all-reduce.3.cloned.1.call-start = ((), (), s32[]{:S(2)}) async-start(), calls=%async_computation.2 | async-start | bytes 16777216
  122.5 3.4 copy-start
  265.2 0.7 copy-start.4
  265.2 1.9 copy-start.2
  265.2 1.9 copy-start.3
  265.2 298.7 %copy-start.1 = (f32[131072]{0:T(1024)S(1)}, f32[131072]{0:T(1024)}, u32[]{:S(2)}) copy-start(f32[131072]{0:T(1024)} %param.15) | copy-start | bytes 1572868
Sparse Core Ops, SparseCore 0:
  9.9 112.6 all-gather.1
  265.3 298.5 all-reduce.2
where the time goes:
time: 584 us; the launch traced here: 576 us
  waiting for transfers between devices  410 us (70%)
  blocking collectives  101 us (17%)
  matrix products  35.7 us (6%)
  between operations  14.7 us (3%)
  local copies, waits for them, and re-layouts  8.41 us (1%)
    unnamed x3, waiting for transfers between devices  297 us
    all_gather x1, waiting for transfers between devices, body(): lax.all_gather(amplitudes, 'gx', axis=0, tiled=True)  113 us
    all_to_all x1, blocking collectives, body(): lax.all_to_all(partial_value, 'gx', split_axis=0, concat_axis=1, tiled=True)  101 us
    dot_general x1, matrix products, body(): jnp.dot(lax.all_gather(amplitudes, 'gx', axis=0, tiled=True), effective,...  34 us
  transfers between devices with their start and end apart: 2, of which 2 were waited for; matrix products, arithmetic and copies ran while one was open for 0% of the time, Pallas kernels for 0%

commit v1 on v0

v1 whole, which is shorter than its diff:
```python
import jax
import jax.numpy as jnp
from jax import lax
from jax.experimental import pallas as pl
from jax.experimental.pallas import tpu as pltpu
from jax.sharding import Mesh, PartitionSpec as P

BLK = 128
TILE = 512
STEP = 256
GX = ("zl", "y", "x", "c")
PLANE = ("y", "x", "c")
Z = ("zl", "row")


def z_shift(value, shift):
    at = [4 * (z % 2) + z // 2 for z in range(8)]
    return lax.ppermute(value, Z, [(at[z], at[(z + shift) % 8]) for z in range(8)])


def ring(axis, value, shift):
    return lax.ppermute(value, axis, [((i + shift) % 4, i) for i in range(4)])


def gate(values, earlier):
    anywhere = pl.BlockSpec(memory_space=pl.ANY)
    return pl.pallas_call(
        lambda *refs: None,
        in_specs=[anywhere] * (len(values) + len(earlier)),
        out_specs=[anywhere] * len(values),
        out_shape=[jax.ShapeDtypeStruct(value.shape, value.dtype) for value in values],
        input_output_aliases={k: k for k in range(len(values))},
        cost_estimate=pl.CostEstimate(flops=0, bytes_accessed=0, transcendentals=0),
    )(*values, *earlier)


def pack(half, place, near, far, earlier):
    cols = near[0].shape[-1]
    chunks = cols // BLK

    def kernel(place_ref, own_n, other_n, own_f, right_f, left_f, *refs):
        out_ref = refs[-1]
        here = lax.rem(pl.program_id(0) - place_ref[0] + 4, 4) == 0
        for i in range(2):
            own = jnp.where(here, own_n[i], own_f[i, 0])
            other = jnp.where(here, other_n[i], right_f[i, 0] + left_f[i, 0])
            for z in range(2):
                value = jnp.where(place_ref[1] == z, own, other)
                for k in range(chunks):
                    out_ref[:, (2 * i + z) * chunks + k, :] = value[:, k * BLK : (k + 1) * BLK]

    near_spec = pl.BlockSpec((2, 8, cols), lambda j, place: (half, 0, 0))
    far_spec = pl.BlockSpec(
        (2, 1, 8, cols), lambda j, place: (0, jnp.maximum(lax.rem(j - place[0] + 4, 4) - 1, 0), 0, 0)
    )
    return pl.pallas_call(
        kernel,
        grid_spec=pltpu.PrefetchScalarGridSpec(
            num_scalar_prefetch=1,
            grid=(4,),
            in_specs=[near_spec] * 2 + [far_spec] * 3 + [pl.BlockSpec(memory_space=pl.ANY)] * len(earlier),
            out_specs=pl.BlockSpec((8, 4 * chunks, BLK), lambda j, place: (j, 0, 0)),
        ),
        out_shape=jax.ShapeDtypeStruct((32, 4 * chunks, BLK), jnp.float32),
        cost_estimate=pl.CostEstimate(flops=0, bytes_accessed=2**20, transcendentals=0),
    )(place, *near, *far, *earlier)


def multiply(pieces, order, integrals, mask_rows, sizes, earlier=()):
    rows = order.shape[0]
    depth, cols = integrals.shape
    tile = min(TILE, cols)
    step = min(STEP, tile)

    def kernel(*refs):
        piece_refs, refs = refs[: len(pieces)], refs[len(pieces) :]
        order_ref, int_ref, mask_ref = refs[:3]
        out_refs, (high_ref, low_ref) = refs[3 + len(earlier) : -2], refs[-2:]

        @pl.when(pl.program_id(0) == 0)
        def _():
            value = jnp.concatenate([ref[...] for ref in piece_refs], axis=0)
            high = value.astype(jnp.bfloat16)
            low = (value - high.astype(jnp.float32)).astype(jnp.bfloat16)
            for part, part_ref in ((high, high_ref), (low, low_ref)):
                moved = jnp.dot(order_ref[...], part, preferred_element_type=jnp.float32)
                part_ref[...] = moved.astype(jnp.bfloat16)

        for start in range(0, tile, step):
            here = slice(start, start + step)
            effective = jnp.concatenate(
                [
                    int_ref[b * BLK : (b + 1) * BLK, here] * mask_ref[b : b + 1, here]
                    for b in range(depth // BLK)
                ],
                axis=0,
            )
            high = effective.astype(jnp.bfloat16)
            low = (effective - high.astype(jnp.float32)).astype(jnp.bfloat16)
            total = jnp.dot(high_ref[...], low, preferred_element_type=jnp.float32)
            total += jnp.dot(low_ref[...], high, preferred_element_type=jnp.float32)
            total += jnp.dot(high_ref[...], high, preferred_element_type=jnp.float32)
            at = 0
            for size, out_ref in zip(sizes, out_refs):
                out_ref[:, here] = total[at : at + size]
                at += size

    return pl.pallas_call(
        kernel,
        grid=(cols // tile,),
        in_specs=[pl.BlockSpec(piece.shape, lambda j: (0, 0)) for piece in pieces]
        + [
            pl.BlockSpec(order.shape, lambda j: (0, 0)),
            pl.BlockSpec((depth, tile), lambda j: (0, j)),
            pl.BlockSpec((mask_rows.shape[0], tile), lambda j: (0, j)),
        ]
        + [pl.BlockSpec(memory_space=pl.ANY)] * len(earlier),
        out_specs=[pl.BlockSpec((size, tile), lambda j: (0, j)) for size in sizes],
        out_shape=[jax.ShapeDtypeStruct((size, cols), jnp.float32) for size in sizes],
        scratch_shapes=[pltpu.VMEM((rows, depth), jnp.bfloat16)] * 2,
        compiler_params=pltpu.CompilerParams(vmem_limit_bytes=56 * 2**20),
        cost_estimate=pl.CostEstimate(
            flops=6 * rows * depth * cols,
            bytes_accessed=4 * (rows * depth + depth * cols + rows * cols),
            transcendentals=0,
        ),
    )(*pieces, order, integrals, mask_rows, *earlier)


def body(amplitudes, integrals, cd_irrep, ab_irrep, allowed, pair_occ, occ_energy, ab_energy):
    zl = lax.axis_index("zl")
    row = lax.axis_index("row")
    y, x, c = lax.axis_index("y"), lax.axis_index("x"), lax.axis_index("c")
    depth = amplitudes.shape[1]
    cols = integrals.shape[1]

    labels = jnp.arange(allowed.shape[0], dtype=jnp.int32)
    cd_hot = (cd_irrep[:, None] == labels[None, :])[:, None, :, None]
    ab_hot = (ab_irrep[:, None] == labels[None, :])[None, :, None, :]
    block_mask = jnp.sum(jnp.where(cd_hot & ab_hot, allowed[None, None], 0), axis=(2, 3)).astype(jnp.float32)
    mask_rows = jnp.repeat(block_mask, BLK, axis=1)

    mine = amplitudes.reshape(4, 2, 2, depth).transpose(1, 0, 2, 3).reshape(2, 8, depth)
    theirs = lax.ppermute(mine, "zl", [(0, 1), (1, 0)])
    flat = jnp.concatenate([mine, theirs], axis=1)
    in_x = jnp.stack([flat] + [ring("x", flat, shift) for shift in (1, 2, 3)], axis=0)

    def other_core(value):
        return lax.ppermute(value, "c", [(0, 1), (1, 0)])

    def order_of(source, total):
        found = source.reshape(-1, 1) == jnp.arange(total, dtype=jnp.int32)[None, :]
        return found.astype(jnp.bfloat16)

    def iotas(*grid):
        return [lax.broadcasted_iota(jnp.int32, grid, k) for k in range(len(grid))]

    def near_order():
        r, s, h, i, _, at_x, at_c = iotas(4, 2, 2, 2, 1, 4, 2)
        piece = jnp.where(at_c == c, 0, 1)
        dx = lax.rem(at_x - x + 4, 4)
        return order_of(((((piece * 4 + dx) * 2 + h) * 2 + s) * 4 + r) * 2 + i, 256)

    def far_order():
        o, i, dy, at_x, at_c = iotas(8, 2, 3, 4, 2)
        steps = [jnp.where(zl == 0, zero, one) for zero, one in ((1, 2), (2, 3), (0, 1), (3, 0))]
        r = o
        for k in range(4):
            r = jnp.where(o == 4 + k, lax.rem(row + steps[k], 4), r)
        s = jnp.where(o < 4, 0, 1)
        piece = jnp.where(at_c == c, 0, 3) + dy
        dx = lax.rem(at_x - x + 4, 4)
        return order_of((((piece * 4 + dx) * 2 + s) * 4 + r) * 2 + i, 384)

    def last_order():
        steps = [jnp.where(zl == 0, zero, one) for zero, one in ((1, 2), (2, 3), (0, 1), (3, 0))]
        groups = (
            [(0, 2, 1), (1, 0, 0), (1, 0, 1), (0, 1, 0)]
            + [(0, 2, 0), (1, 1, 0), (1, 1, 1), (0, 3, 1)]
            + [(0, 1, 1), (1, 2, 0), (1, 2, 1)]
            + [(0, 3, 0), (1, 3, 0), (1, 3, 1)]
            + [(0, 0, 0), (0, 0, 1)]
        )
        starts = [
            (s * 4 + lax.rem(row + (steps[k] if s else k), 4)) * 2 + i for s, k, i in groups
        ]
        start = jnp.stack(starts).astype(jnp.int32).reshape(16, 1, 1, 1)
        _, dy, at_x, at_c = iotas(16, 3, 4, 2)
        piece = jnp.where(at_c == c, 0, 3) + dy
        return order_of((piece * 4 + lax.rem(at_x - x + 4, 4)) * 16 + start, 384)

    def product(pieces, order, sizes, *earlier):
        return multiply(pieces, order, integrals, mask_rows, sizes, earlier)

    def own_sum(part):
        return lax.psum_scatter(part[0], "row", scatter_dimension=0, tiled=True)

    def first_stage(part):
        return z_shift(part[1], 2), z_shift(part[2], -2)

    def second_stage(part, got):
        return z_shift(part[3] + got[0], 1), z_shift(part[4] + got[1], -1)

    def packed(half, near_sums, far_sums, earlier=()):
        near_sums = [value.reshape(4, 8, cols) for value in near_sums]
        far_sums = [value.reshape(2, 3, 8, cols) for value in far_sums]
        return pack(half, jnp.stack([y, zl]).astype(jnp.int32), near_sums, far_sums, earlier)

    def to_owners(sent):
        return lax.all_to_all(sent, PLANE, 0, 0, tiled=True)

    pieces = in_x.reshape(128, depth)
    part_near = product([pieces, other_core(pieces)], near_order(), (256,))
    sum_near = own_sum(part_near)
    sums_near = (sum_near[:32], lax.ppermute(sum_near[32:], "zl", [(0, 1), (1, 0)]))

    order = far_order()
    sizes = (192, 48, 48, 48, 48)

    def gathered(half, before, after):
        pieces = in_x[:, half].reshape(64, depth)
        if before:
            (pieces,) = gate([pieces], before)
        pieces = list(gate([ring("y", pieces, shift) for shift in (1, 2, 3)], after))
        return pieces + [other_core(value) for value in pieces]

    far_a = gathered(0, (), part_near)
    part_a = product(far_a, order, sizes)
    own_a = own_sum(part_a)
    first_a = first_stage(part_a)

    far_b = gathered(1, far_a[:3], part_a[1:2])
    part_b = product(far_b, last_order(), (96, 96, 72, 72, 48), *first_a)
    first_b = first_stage((None, *part_b[:2]))
    out_a = to_owners(packed(0, sums_near, (own_a,) + second_stage(part_a, first_a), first_b))

    right, left = first_b
    to_right = part_b[2] + right[:72]
    to_left = part_b[3] + left[:72]
    relay_right, cross_right = z_shift(to_right[:24], 2), z_shift(to_right[24:], 1)
    relay_left, cross_left = z_shift(to_left[:24], -2), z_shift(to_left[24:], -1)
    own_b = jnp.concatenate(
        [part_b[4][:24] + right[72:] + relay_left, part_b[4][24:] + left[72:] + relay_right], axis=0
    )
    out_b = to_owners(packed(1, sums_near, (own_b, cross_right, cross_left)))
    out = [
        got.reshape(32, 2, 2, cols).transpose(1, 2, 0, 3).reshape(2, 64 * cols) for got in (out_a, out_b)
    ]

    residual = jnp.concatenate(out, axis=0)
    occ_labels = jnp.arange(occ_energy.shape[0], dtype=jnp.int32)
    pair_hot = (pair_occ[:, :, None] == occ_labels[None, None, :]).astype(jnp.float32)
    pair_energy = jnp.sum(pair_hot * occ_energy[None, None, :], axis=(1, 2))
    update = residual / (ab_energy[None, :] - pair_energy[:, None])
    return (residual, update)


def solution(mesh):
    fine = Mesh(mesh.devices.reshape(2, 4, 4, 2, 4), GX + ("row",))
    return jax.shard_map(
        body,
        mesh=fine,
        in_specs=(
            P(GX, "row"),
            P("row", GX),
            P("row"),
            P(GX),
            P(),
            P(GX + ("row",), None),
            P(),
            P(),
        ),
        out_specs=(P(GX + ("row",), None), P(GX + ("row",), None)),
        check_vma=False,
    )
```

time: 584 us -> 272 us (0.47); the launches traced: 576 us -> 271 us
  waiting for transfers between devices: 410 us -> 123 us
  blocking collectives: 101 us -> 0 us
  starting transfers between devices: 0.08 us -> 62.5 us
  Pallas kernels: 0 us -> 38 us
  matrix products: 35.7 us -> 0 us
  local copies, waits for them, and re-layouts: 8.41 us -> 18.9 us
  other arithmetic: 5.17 us -> 13.9 us
    unnamed x3 -> x2, waiting for transfers between devices: 297 us -> 0.03 us
    all_gather x1 -> x0, waiting for transfers between devices: 113 us -> none  [body(): lax.all_gather(amplitudes, 'gx', axis=0, tiled=True)]
    ppermute x0 -> x28, waiting for transfers between devices: none -> 108 us  [the longest x10 80.4 us: z_shift(): lax.ppermute(value, Z, [(at[z], at[(z + shift) % 8]) for z in range(8)])]
    all_to_all x1 -> x0, blocking collectives: 101 us -> none  [body(): lax.all_to_all(partial_value, 'gx', split_axis=0, concat_axis=1, tiled=True)]
    ppermute x0 -> x28, starting transfers between devices: none -> 45.8 us  [the longest x10 22.2 us: z_shift(): lax.ppermute(value, Z, [(at[z], at[(z + shift) % 8]) for z in range(8)])]
    pallas_call x0 -> x8, Pallas kernels: none -> 38 us  [the longest x3 28.6 us: multiply(): pl.pallas_call(kernel, grid=(cols // tile,), in_specs=[pl.BlockSpec(piece...]
    dot_general x3 -> x0, matrix products: 35.7 us -> none  [the longest x1 34 us: body(): jnp.dot(lax.all_gather(amplitudes, 'gx', axis=0, tiled=True), effective,...]
    all_to_all x0 -> x2, starting transfers between devices: none -> 16.6 us  [to_owners(): return lax.all_to_all(sent, PLANE, 0, 0, tiled=True)]
  transfers between devices with their start and end apart: 2 -> 32, of which waited for: 2 -> 17; matrix products, arithmetic and copies ran while one was open for 0% -> 7% of each run, Pallas kernels for 0% -> 11%
where the time goes in v1:
time: 272 us; the launch traced here: 271 us
  waiting for transfers between devices  123 us (45%)
  starting transfers between devices  62.5 us (23%)
  Pallas kernels  38 us (14%)
  local copies, waits for them, and re-layouts  18.9 us (7%)
  between operations  14.6 us (5%)
  other arithmetic  13.9 us (5%)
    ppermute x10, waiting for transfers between devices, z_shift(): lax.ppermute(value, Z, [(at[z], at[(z + shift) % 8]) for z in range(8)])  80.4 us
    pallas_call x3, Pallas kernels, multiply(): pl.pallas_call(kernel, grid=(cols // tile,), in_specs=[pl.BlockSpec(piece...  28.6 us
    ppermute x10, starting transfers between devices, z_shift(): lax.ppermute(value, Z, [(at[z], at[(z + shift) % 8]) for z in range(8)])  22.2 us
    ppermute x9, waiting for transfers between devices, ring(): return lax.ppermute(value, axis, [((i + shift) % 4, i) for i in range(4)])  20.5 us
    all_to_all x2, starting transfers between devices, to_owners(): return lax.all_to_all(sent, PLANE, 0, 0, tiled=True)  16.6 us
    all_to_all x2, waiting for transfers between devices, to_owners(): return lax.all_to_all(sent, PLANE, 0, 0, tiled=True)  15 us
    ppermute x9, starting transfers between devices, ring(): return lax.ppermute(value, axis, [((i + shift) % 4, i) for i in range(4)])  13.4 us
    pallas_call x2, Pallas kernels, pack(): pl.pallas_call(kernel, grid_spec=pltpu.PrefetchScalarGridSpec(num_scalar_...  9.43 us
  transfers between devices with their start and end apart: 32, of which 17 were waited for; matrix products, arithmetic and copies ran while one was open for 7% of the time, Pallas kernels for 11%

profile of v1, /device:TPU:1, one launch (start us, length us, event | category | flops | bytes accessed | tf_op | source)
XLA Modules:
  0.0 270.8 jit_solution(16160394308242288384)
XLA Ops:
  18.9 3.3 %collective-permute-done.2 = f32[2,16,1024]{2,1,0:T(8,128)S(1)} collective-permute-done((f32[2,16,1024]{2,1,0:T(8,128)S(1)}, f32[2,16,1024]{2,1,0:T(8,128)S(1)}, u32[]{:S(2)}, u32[]{:S(2)}) %collective-permute-start.2) | collective-permute-done | bytes 131104 | tf_op jit(solution)/shard_map/ppermute | solution.py:22
  27.1 8.2 %shard_map.95.refs_3_ = f32[256,2048]{1,0:T(8,128)} custom-call(f32[128,1024]{1,0:T(8,128)} %bitcast.74, f32[128,1024]{1,0:T(8,128)} %copy-done.27, bf16[256,256]{1,0:T(8,128)(2,1)} %fusion.2.refs_2_, f32[1024,2048]{1,0:T(8,128)} %refs_7_.3, f32[8,2048]{1,0:T(8,128)} %broadcast_bitcast_fusion.refs_4_.refs_8_), custom_call_target="tpu_custom_call" | custom-call | flops 3221225472 | bytes 11534336 | tf_op jit(solution)/shard_map/pallas_call | solution.py:108
  37.4 2.6 collective-permute-start.7
  42.0 3.0 %collective-permute-done.8.refs_2_ = f32[64,1024]{1,0:T(8,128)S(1)} collective-permute-done((f32[64,1024]{1,0:T(8,128)S(1)}, f32[64,1024]{1,0:T(8,128)S(1)}, u32[]{:S(2)}, u32[]{:S(2)}) %collective-permute-start.8) | collective-permute-done | bytes 262176 | tf_op jit(solution)/shard_map/ppermute | solution.py:22
  45.0 6.6 %collective-permute-done.7.refs_1_ = f32[64,1024]{1,0:T(8,128)S(1)} collective-permute-done((f32[64,1024]{1,0:T(8,128)S(1)}, f32[64,1024]{1,0:T(8,128)S(1)}, u32[]{:S(2)}, u32[]{:S(2)}) %collective-permute-start.7) | collective-permute-done | bytes 262176 | tf_op jit(solution)/shard_map/ppermute | solution.py:22
  57.4 10.2 %shard_map.97 = (f32[192,2048]{1,0:T(8,128)}, f32[48,2048]{1,0:T(8,128)}, f32[48,2048]{1,0:T(8,128)}, f32[48,2048]{1,0:T(8,128)}, f32[48,2048]{1,0:T(8,128)}) custom-call(f32[64,1024]{1,0:T(8,128)} %get-tuple-element.18.refs_0_.refs_1_, f32[64,1024]{1,0:T(8,128)} %get-tuple-element.19.refs_1_.refs_2_, f32[64,1024]{1,0:T(8,128)} %get-tuple-element.20.refs_2_.refs_3_, ...), custom_call_target="tpu_custom_call" | custom-call | flops 4831838208 | bytes 13107200 | tf_op jit(solution)/shard_map/pallas_call | solution.py:108
  72.2 3.1 %collective-permute-start.12 = (f32[48,2048]{1,0:T(8,128)S(1)}, f32[48,2048]{1,0:T(8,128)S(1)}, u32[]{:S(2)}, u32[]{:S(2)}) collective-permute-start(f32[48,2048]{1,0:T(8,128)S(1)} %copy-done.14), channel_id=1, source_target_pairs={{0,1},{128,129},{1,2},{129,130},{2,3},{130,131},{3,0},{131,128},{4... | collective-permute-start | bytes 1179656 | tf_op jit(solution)/shard_map/ppermute | solution.py:18
  77.2 5.0 %collective-permute-done.17.refs_1_ = f32[64,1024]{1,0:T(8,128)S(1)} collective-permute-done((f32[64,1024]{1,0:T(8,128)}, f32[64,1024]{1,0:T(8,128)S(1)}, u32[]{:S(2)}, u32[]{:S(2)}) %collective-permute-start.17) | collective-permute-done | bytes 262176 | tf_op jit(solution)/shard_map/ppermute | solution.py:22
  85.6 5.1 %collective-permute-start.14 = (f32[48,2048]{1,0:T(8,128)S(1)}, f32[48,2048]{1,0:T(8,128)S(1)}, u32[]{:S(2)}, u32[]{:S(2)}) collective-permute-start(f32[48,2048]{1,0:T(8,128)S(1)} %copy-done.28), channel_id=1, source_target_pairs={{0,3},{128,131},{1,0},{129,128},{2,1},{130,129},{3,2},{131,130},{4... | collective-permute-start | bytes 1179656 | tf_op jit(solution)/shard_map/ppermute | solution.py:18
  91.7 14.8 %collective-permute-done.14.refs_10_ = f32[48,2048]{1,0:T(8,128)S(1)} collective-permute-done((f32[48,2048]{1,0:T(8,128)S(1)}, f32[48,2048]{1,0:T(8,128)S(1)}, u32[]{:S(2)}, u32[]{:S(2)}) %collective-permute-start.14) | collective-permute-done | bytes 393248 | tf_op jit(solution)/shard_map/ppermute | solution.py:18
  107.9 10.2 %shard_map.100 = (f32[96,2048]{1,0:T(8,128)}, f32[96,2048]{1,0:T(8,128)}, f32[72,2048]{1,0:T(8,128)}, f32[72,2048]{1,0:T(8,128)}, f32[48,2048]{1,0:T(8,128)}) custom-call(f32[64,1024]{1,0:T(8,128)} %get-tuple-element.26.refs_0_, f32[64,1024]{1,0:T(8,128)} %get-tuple-element.27.refs_1_, f32[64,1024]{1,0:T(8,128)} %get-tuple-element.28.refs_2_, ...), custom_call_target="tpu_custom_call" | custom-call | flops 4831838208 | bytes 13107200 | tf_op jit(solution)/shard_map/pallas_call | solution.py:108
  118.1 3.7 %collective-permute-start.22 = (f32[96,2048]{1,0:T(8,128)}, f32[96,2048]{1,0:T(8,128)S(1)}, u32[]{:S(2)}, u32[]{:S(2)}) collective-permute-start(f32[96,2048]{1,0:T(8,128)} %get-tuple-element.29), channel_id=1, source_target_pairs={{0,1},{128,129},{1,2},{129,130},{2,3},{130,131},{3,0},{131,128},{4... | collective-permute-start | bytes 2359304 | tf_op jit(solution)/shard_map/ppermute | solution.py:18
  133.1 39.3 %collective-permute-done.22.refs_0_ = f32[96,2048]{1,0:T(8,128)S(1)} collective-permute-done((f32[96,2048]{1,0:T(8,128)}, f32[96,2048]{1,0:T(8,128)S(1)}, u32[]{:S(2)}, u32[]{:S(2)}) %collective-permute-start.22) | collective-permute-done | bytes 786464 | tf_op jit(solution)/shard_map/ppermute | solution.py:18
  173.2 14.3 %collective-permute-done.13 = f32[48,2048]{1,0:T(8,128)} collective-permute-done((f32[48,2048]{1,0:T(8,128)}, f32[48,2048]{1,0:T(8,128)}, u32[]{:S(2)}, u32[]{:S(2)}) %collective-permute-start.13) | collective-permute-done | bytes 393248 | tf_op jit(solution)/shard_map/ppermute | solution.py:18
  187.5 5.6 %collective-permute-done.5 = f32[32,2048]{1,0:T(8,128)S(1)} collective-permute-done((f32[32,2048]{1,0:T(8,128)}, f32[32,2048]{1,0:T(8,128)S(1)}, u32[]{:S(2)}, u32[]{:S(2)}) %collective-permute-start.5) | collective-permute-done | bytes 262176 | tf_op jit(solution)/shard_map/ppermute | solution.py:215
  193.8 4.7 %shard_map.101 = f32[32,64,128]{2,1,0:T(8,128)} custom-call(s32[2]{0:T(128)} %pad_add_fusion.place_ref, f32[4,8,2048]{2,1,0:T(8,128)} %get-tuple-element.39.own_n, f32[4,8,2048]{2,1,0:T(8,128)} %bitcast.70, f32[2,3,8,2048]{3,2,1,0:T(8,128)} %bitcast.75, f32[2,3,8,2048]{3,2,1,0:T(8,128)} %bitcast.16.right_f, f32[2,3,8,2048]{3,2,1,0:T(8,128)} %bitcast.76, ...), custom_call_target="tpu_custom_call" | custom-call | bytes 1048576 | tf_op jit(solution)/shard_map/pallas_call | solution.py:56
  198.5 8.8 %all-to-all-start = ((f32[32,64,128]{2,1,0:T(8,128)}), f32[32,64,128]{2,1,0:T(8,128)S(1)}, u32[]{:S(2)}, u32[]{:S(2)}) async-start(f32[32,64,128]{2,1,0:T(8,128)} %shard_map.101), calls=%async_computation.2 | async-start | bytes 2097152 | tf_op jit(solution)/shard_map/all_to_all | solution.py:210
  207.4 3.1 %collective-permute-start.24 = (f32[24,2048]{1,0:T(8,128)S(1)}, f32[24,2048]{1,0:T(8,128)S(1)}, u32[]{:S(2)}, u32[]{:S(2)}) collective-permute-start(f32[24,2048]{1,0:T(8,128)S(1)} %slice.62), channel_id=1, source_target_pairs={{0,3},{128,131},{1,0},{129,128},{2,1},{130,129},{3,2},{131,130},{4... | collective-permute-start | bytes 589832 | tf_op jit(solution)/shard_map/ppermute | solution.py:18
  218.4 4.6 %collective-permute-done.26 = f32[48,2048]{1,0:T(8,128)S(1)} collective-permute-done((f32[48,2048]{1,0:T(8,128)S(1)}, f32[48,2048]{1,0:T(8,128)S(1)}, u32[]{:S(2)}, u32[]{:S(2)}) %collective-permute-start.26) | collective-permute-done | bytes 393248 | tf_op jit(solution)/shard_map/ppermute | solution.py:18
  223.0 5.1 %collective-permute-done.27 = f32[48,2048]{1,0:T(8,128)S(1)} collective-permute-done((f32[48,2048]{1,0:T(8,128)S(1)}, f32[48,2048]{1,0:T(8,128)S(1)}, u32[]{:S(2)}, u32[]{:S(2)}) %collective-permute-start.27) | collective-permute-done | bytes 393248 | tf_op jit(solution)/shard_map/ppermute | solution.py:18
  228.8 4.8 %shard_map.102 = f32[32,64,128]{2,1,0:T(8,128)} custom-call(s32[2]{0:T(128)} %pad_add_fusion.place_ref, f32[4,8,2048]{2,1,0:T(8,128)} %get-tuple-element.39.own_n, f32[4,8,2048]{2,1,0:T(8,128)} %bitcast.71, f32[2,3,8,2048]{3,2,1,0:T(8,128)} %bitcast.69, f32[2,3,8,2048]{3,2,1,0:T(8,128)} %bitcast.77, f32[2,3,8,2048]{3,2,1,0:T(8,128)} %bitcast.78), custom_call_target="tpu_custom_call" | custom-call | bytes 1048576 | tf_op jit(solution)/shard_map/pallas_call | solution.py:56
  233.6 7.9 %all-to-all-start.1 = ((f32[32,64,128]{2,1,0:T(8,128)}), f32[32,64,128]{2,1,0:T(8,128)S(1)}, u32[]{:S(2)}, u32[]{:S(2)}) async-start(f32[32,64,128]{2,1,0:T(8,128)} %shard_map.102), calls=%async_computation.3 | async-start | bytes 2097152 | tf_op jit(solution)/shard_map/all_to_all | solution.py:210
  243.7 15.0 %all-to-all-done.1 = f32[32,64,128]{2,1,0:T(8,128)S(1)} async-done(((f32[32,64,128]{2,1,0:T(8,128)}), f32[32,64,128]{2,1,0:T(8,128)S(1)}, u32[]{:S(2)}, u32[]{:S(2)}) %all-to-all-start.1) | async-done | bytes 1048608 | tf_op jit(solution)/shard_map/all_to_all | solution.py:210
  260.7 3.3 %subtract_divide_fusion = (f32[4,131072]{1,0:T(4,128)}, f32[4,131072]{1,0:T(4,128)}) fusion(f32[4]{0:T(128)S(1)} %select_reduce_fusion.1, f32[131072]{0:T(1024)S(1)} %copy-done.10, f32[2,131072]{1,0:T(2,128)S(1)} %bitcast.68, f32[2,131072]{1,0:T(2,128)S(1)} %bitcast.67), kind=kLoop, calls=%fused_computation.1 | loop fusion | flops 1572864 | bytes 6815760 | tf_op jit(solution)/shard_map/div | solution.py:254
  (194 shorter events, 64.3 us)
Async XLA Ops:
  7.2 122.5 %reduce-scatter.3.cloned.1.call-start = ((), (), s32[]{:S(2)}) async-start(), calls=%async_computation.4 | async-start | bytes 2621440 | tf_op jit(solution)/shard_map/reduce_scatter | solution.py:196
  14.6 7.5 %collective-permute-start.2 = (f32[2,16,1024]{2,1,0:T(8,128)S(1)}, f32[2,16,1024]{2,1,0:T(8,128)S(1)}, u32[]{:S(2)}, u32[]{:S(2)}) collective-permute-start(f32[2,16,1024]{2,1,0:T(8,128)S(1)} %constant_dynamic-update-slice_fusion), channel_id=1, source_target_pairs={{16,0},{24,8},{0,16},{8,24},{17,1},{25,9},{1,17},{9,25},{18,2},{26... | collective-permute-start | bytes 393224 | tf_op jit(solution)/shard_map/ppermute | solution.py:22
  35.3 152.1 %reduce-scatter.5.cloned.1.call-start = ((), (), s32[]{:S(2)}) async-start(), calls=%async_computation.5 | async-start | bytes 1966080 | tf_op jit(solution)/shard_map/reduce_scatter | solution.py:196
  36.3 8.7 %collective-permute-start.8 = (f32[64,1024]{1,0:T(8,128)S(1)}, f32[64,1024]{1,0:T(8,128)S(1)}, u32[]{:S(2)}, u32[]{:S(2)}) collective-permute-start(f32[64,1024]{1,0:T(8,128)S(1)} %bitcast.81), channel_id=1, source_target_pairs={{96,0},{0,32},{32,64},{64,96},{97,1},{1,33},{33,65},{65,97},{98,2}... | collective-permute-start | bytes 786440 | tf_op jit(solution)/shard_map/ppermute | solution.py:22
  37.4 14.3 %collective-permute-start.7 = (f32[64,1024]{1,0:T(8,128)S(1)}, f32[64,1024]{1,0:T(8,128)S(1)}, u32[]{:S(2)}, u32[]{:S(2)}) collective-permute-start(f32[64,1024]{1,0:T(8,128)S(1)} %bitcast.82), channel_id=1, source_target_pairs={{64,0},{96,32},{0,64},{32,96},{65,1},{97,33},{1,65},{33,97},{66,2}... | collective-permute-start | bytes 786440 | tf_op jit(solution)/shard_map/ppermute | solution.py:22
  40.0 11.7 %collective-permute-start.6 = (f32[64,1024]{1,0:T(8,128)S(1)}, f32[64,1024]{1,0:T(8,128)S(1)}, u32[]{:S(2)}, u32[]{:S(2)}) collective-permute-start(f32[64,1024]{1,0:T(8,128)S(1)} %bitcast.83), channel_id=1, source_target_pairs={{32,0},{64,32},{96,64},{0,96},{33,1},{65,33},{97,65},{1,97},{34,2}... | collective-permute-start | bytes 786440 | tf_op jit(solution)/shard_map/ppermute | solution.py:22
  67.7 9.5 %collective-permute-start.18 = (f32[64,1024]{1,0:T(8,128)}, f32[64,1024]{1,0:T(8,128)S(1)}, u32[]{:S(2)}, u32[]{:S(2)}) collective-permute-start(f32[64,1024]{1,0:T(8,128)} %shard_map.98), channel_id=1, source_target_pairs={{96,0},{0,32},{32,64},{64,96},{97,1},{1,33},{33,65},{65,97},{98,2}... | collective-permute-start | bytes 786440 | tf_op jit(solution)/shard_map/ppermute | solution.py:22
  68.1 14.1 %collective-permute-start.17 = (f32[64,1024]{1,0:T(8,128)}, f32[64,1024]{1,0:T(8,128)S(1)}, u32[]{:S(2)}, u32[]{:S(2)}) collective-permute-start(f32[64,1024]{1,0:T(8,128)} %shard_map.98), channel_id=1, source_target_pairs={{64,0},{96,32},{0,64},{32,96},{65,1},{97,33},{1,65},{33,97},{66,2}... | collective-permute-start | bytes 786440 | tf_op jit(solution)/shard_map/ppermute | solution.py:22
  70.2 12.6 %collective-permute-start.16 = (f32[64,1024]{1,0:T(8,128)}, f32[64,1024]{1,0:T(8,128)S(1)}, u32[]{:S(2)}, u32[]{:S(2)}) collective-permute-start(f32[64,1024]{1,0:T(8,128)} %shard_map.98), channel_id=1, source_target_pairs={{32,0},{64,32},{96,64},{0,96},{33,1},{65,33},{97,65},{1,97},{34,2}... | collective-permute-start | bytes 786440 | tf_op jit(solution)/shard_map/ppermute | solution.py:22
  72.2 34.3 %collective-permute-start.12 = (f32[48,2048]{1,0:T(8,128)S(1)}, f32[48,2048]{1,0:T(8,128)S(1)}, u32[]{:S(2)}, u32[]{:S(2)}) collective-permute-start(f32[48,2048]{1,0:T(8,128)S(1)} %copy-done.14), channel_id=1, source_target_pairs={{0,1},{128,129},{1,2},{129,130},{2,3},{130,131},{3,0},{131,128},{4... | collective-permute-start | bytes 1179656 | tf_op jit(solution)/shard_map/ppermute | solution.py:18
  83.6 8.0 %collective-permute-start.19 = (f32[64,1024]{1,0:T(8,128)}, f32[64,1024]{1,0:T(8,128)S(1)}, u32[]{:S(2)}, u32[]{:S(2)}) collective-permute-start(f32[64,1024]{1,0:T(8,128)} %get-tuple-element.26.refs_0_), channel_id=1, source_target_pairs={{0,4},{4,0},{1,5},{5,1},{2,6},{6,2},{3,7},{7,3},{8,12},{12,8},{9,1... | collective-permute-start | bytes 786440 | tf_op jit(solution)/shard_map/ppermute | solution.py:149
  85.1 6.5 %collective-permute-start.21 = (f32[64,1024]{1,0:T(8,128)}, f32[64,1024]{1,0:T(8,128)S(1)}, u32[]{:S(2)}, u32[]{:S(2)}) collective-permute-start(f32[64,1024]{1,0:T(8,128)} %get-tuple-element.28.refs_2_), channel_id=1, source_target_pairs={{0,4},{4,0},{1,5},{5,1},{2,6},{6,2},{3,7},{7,3},{8,12},{12,8},{9,1... | collective-permute-start | bytes 786440 | tf_op jit(solution)/shard_map/ppermute | solution.py:149
  85.6 20.9 %collective-permute-start.14 = (f32[48,2048]{1,0:T(8,128)S(1)}, f32[48,2048]{1,0:T(8,128)S(1)}, u32[]{:S(2)}, u32[]{:S(2)}) collective-permute-start(f32[48,2048]{1,0:T(8,128)S(1)} %copy-done.28), channel_id=1, source_target_pairs={{0,3},{128,131},{1,0},{129,128},{2,1},{130,129},{3,2},{131,130},{4... | collective-permute-start | bytes 1179656 | tf_op jit(solution)/shard_map/ppermute | solution.py:18
  118.1 54.2 %collective-permute-start.22 = (f32[96,2048]{1,0:T(8,128)}, f32[96,2048]{1,0:T(8,128)S(1)}, u32[]{:S(2)}, u32[]{:S(2)}) collective-permute-start(f32[96,2048]{1,0:T(8,128)} %get-tuple-element.29), channel_id=1, source_target_pairs={{0,1},{128,129},{1,2},{129,130},{2,3},{130,131},{3,0},{131,128},{4... | collective-permute-start | bytes 2359304 | tf_op jit(solution)/shard_map/ppermute | solution.py:18
  124.2 49.0 %collective-permute-start.15 = (f32[48,2048]{1,0:T(8,128)}, f32[48,2048]{1,0:T(8,128)S(1)}, u32[]{:S(2)}, u32[]{:S(2)}) collective-permute-start(f32[48,2048]{1,0:T(8,128)} %add.259), channel_id=1, source_target_pairs={{0,131},{128,0},{1,128},{129,1},{2,129},{130,2},{3,130},{131,3},{4... | collective-permute-start | bytes 1179656 | tf_op jit(solution)/shard_map/ppermute | solution.py:18
  127.3 60.1 %collective-permute-start.13 = (f32[48,2048]{1,0:T(8,128)}, f32[48,2048]{1,0:T(8,128)}, u32[]{:S(2)}, u32[]{:S(2)}) collective-permute-start(f32[48,2048]{1,0:T(8,128)} %add.258), channel_id=1, source_target_pairs={{0,128},{128,1},{1,129},{129,2},{2,130},{130,3},{3,131},{131,0},{4... | collective-permute-start | bytes 1179656 | tf_op jit(solution)/shard_map/ppermute | solution.py:18
  127.5 60.0 %collective-permute-start.23 = (f32[96,2048]{1,0:T(8,128)}, f32[96,2048]{1,0:T(8,128)S(1)}, u32[]{:S(2)}, u32[]{:S(2)}) collective-permute-start(f32[96,2048]{1,0:T(8,128)} %get-tuple-element.30), channel_id=1, source_target_pairs={{0,3},{128,131},{1,0},{129,128},{2,1},{130,129},{3,2},{131,130},{4... | collective-permute-start | bytes 2359304 | tf_op jit(solution)/shard_map/ppermute | solution.py:18
  131.5 61.5 %collective-permute-start.5 = (f32[32,2048]{1,0:T(8,128)}, f32[32,2048]{1,0:T(8,128)S(1)}, u32[]{:S(2)}, u32[]{:S(2)}) collective-permute-start(f32[32,2048]{1,0:T(8,128)} %get-tuple-element.38), channel_id=1, source_target_pairs={{0,128},{128,0},{1,129},{129,1},{2,130},{130,2},{3,131},{131,3},{4... | collective-permute-start | bytes 786440 | tf_op jit(solution)/shard_map/ppermute | solution.py:215
  173.2 40.9 %collective-permute-start.25 = (f32[24,2048]{1,0:T(8,128)}, f32[24,2048]{1,0:T(8,128)S(1)}, u32[]{:S(2)}, u32[]{:S(2)}) collective-permute-start(f32[24,2048]{1,0:T(8,128)} %slice.65), channel_id=1, source_target_pairs={{0,1},{128,129},{1,2},{129,130},{2,3},{130,131},{3,0},{131,128},{4... | collective-permute-start | bytes 589832 | tf_op jit(solution)/shard_map/ppermute | solution.py:18
  198.5 35.2 %all-to-all-start = ((f32[32,64,128]{2,1,0:T(8,128)}), f32[32,64,128]{2,1,0:T(8,128)S(1)}, u32[]{:S(2)}, u32[]{:S(2)}) async-start(f32[32,64,128]{2,1,0:T(8,128)} %shard_map.101), calls=%async_computation.2 | async-start | bytes 2097152 | tf_op jit(solution)/shard_map/all_to_all | solution.py:210
  207.4 9.1 %collective-permute-start.24 = (f32[24,2048]{1,0:T(8,128)S(1)}, f32[24,2048]{1,0:T(8,128)S(1)}, u32[]{:S(2)}, u32[]{:S(2)}) collective-permute-start(f32[24,2048]{1,0:T(8,128)S(1)} %slice.62), channel_id=1, source_target_pairs={{0,3},{128,131},{1,0},{129,128},{2,1},{130,129},{3,2},{131,130},{4... | collective-permute-start | bytes 589832 | tf_op jit(solution)/shard_map/ppermute | solution.py:18
  210.5 12.5 %collective-permute-start.26 = (f32[48,2048]{1,0:T(8,128)S(1)}, f32[48,2048]{1,0:T(8,128)S(1)}, u32[]{:S(2)}, u32[]{:S(2)}) collective-permute-start(f32[48,2048]{1,0:T(8,128)S(1)} %slice.66), channel_id=1, source_target_pairs={{0,128},{128,1},{1,129},{129,2},{2,130},{130,3},{3,131},{131,0},{4... | collective-permute-start | bytes 1179656 | tf_op jit(solution)/shard_map/ppermute | solution.py:18
  212.7 15.4 %collective-permute-start.27 = (f32[48,2048]{1,0:T(8,128)S(1)}, f32[48,2048]{1,0:T(8,128)S(1)}, u32[]{:S(2)}, u32[]{:S(2)}) collective-permute-start(f32[48,2048]{1,0:T(8,128)S(1)} %slice.67), channel_id=1, source_target_pairs={{0,131},{128,0},{1,128},{129,1},{2,129},{130,2},{3,130},{131,3},{4... | collective-permute-start | bytes 1179656 | tf_op jit(solution)/shard_map/ppermute | solution.py:18
  233.6 25.1 %all-to-all-start.1 = ((f32[32,64,128]{2,1,0:T(8,128)}), f32[32,64,128]{2,1,0:T(8,128)S(1)}, u32[]{:S(2)}, u32[]{:S(2)}) async-start(f32[32,64,128]{2,1,0:T(8,128)} %shard_map.102), calls=%async_computation.3 | async-start | bytes 2097152 | tf_op jit(solution)/shard_map/all_to_all | solution.py:210
  (43 other events, 368.8 us)
Sparse Core Ops, SparseCore 0:
  35.4 65.7 reduce-scatter.2
  104.5 56.4 reduce-scatter.4

commit v2 on v1

--- a/solution.py
+++ b/solution.py
@@ -230,9 +230,11 @@
     first_a = first_stage(part_a)
 
     far_b = gathered(1, far_a[:3], part_a[1:2])
-    part_b = product(far_b, last_order(), (96, 96, 72, 72, 48), *first_a)
+    second_a = second_stage(part_a, first_a)
+    part_b = product(far_b, last_order(), (96, 96, 72, 72, 48), *second_a, sums_near[1])
     first_b = first_stage((None, *part_b[:2]))
-    out_a = to_owners(packed(0, sums_near, (own_a,) + second_stage(part_a, first_a), first_b))
+    sent_a = packed(0, sums_near, (own_a,) + second_a)
+    out_a = to_owners(sent_a)
 
     right, left = first_b
     to_right = part_b[2] + right[:72]

time: 272 us -> 247 us (0.908)
  waiting for transfers between devices: 123 us -> 106 us
  other arithmetic: 13.9 us -> 10.5 us
    ppermute x10, waiting for transfers between devices: 80.4 us -> 26.4 us  [z_shift(): lax.ppermute(value, Z, [(at[z], at[(z + shift) % 8]) for z in range(8)])]
    reduce_scatter x2, waiting for transfers between devices: 0.01 us -> 36.4 us  [own_sum(): return lax.psum_scatter(part[0], 'row', scatter_dimension=0, tiled=True)]
    add x2, other arithmetic: 3.59 us -> 0.09 us  [second_stage(): return (z_shift(part[3] + got[0], 1), z_shift(part[4] + got[1], -1))]
    ppermute x9, waiting for transfers between devices: 20.5 us -> 23.4 us  [ring(): return lax.ppermute(value, axis, [((i + shift) % 4, i) for i in range(4)])]
    unnamed x73 -> x57, local copies, waits for them, and re-layouts: 8.72 us -> 7.13 us
  transfers between devices with their start and end apart: 32 -> 32, of which waited for: 17 -> 19; matrix products, arithmetic and copies ran while one was open for 7% -> 6% of each run, Pallas kernels for 11% -> 12%
where the time goes in v2:
time: 247 us; the launch traced here: 246 us
  waiting for transfers between devices  106 us (43%)
  starting transfers between devices  60.7 us (25%)
  Pallas kernels  37.9 us (15%)
  local copies, waits for them, and re-layouts  16.4 us (7%)
  between operations  14.6 us (6%)
  other arithmetic  10.5 us (4%)
    reduce_scatter x2, waiting for transfers between devices, own_sum(): return lax.psum_scatter(part[0], 'row', scatter_dimension=0, tiled=True)  36.4 us
    pallas_call x3, Pallas kernels, multiply(): pl.pallas_call(kernel, grid=(cols // tile,), in_specs=[pl.BlockSpec(piece...  28.5 us
    ppermute x10, waiting for transfers between devices, z_shift(): lax.ppermute(value, Z, [(at[z], at[(z + shift) % 8]) for z in range(8)])  26.4 us
    ppermute x9, waiting for transfers between devices, ring(): return lax.ppermute(value, axis, [((i + shift) % 4, i) for i in range(4)])  23.4 us
    ppermute x10, starting transfers between devices, z_shift(): lax.ppermute(value, Z, [(at[z], at[(z + shift) % 8]) for z in range(8)])  21.9 us
    all_to_all x2, starting transfers between devices, to_owners(): return lax.all_to_all(sent, PLANE, 0, 0, tiled=True)  15.8 us
    all_to_all x2, waiting for transfers between devices, to_owners(): return lax.all_to_all(sent, PLANE, 0, 0, tiled=True)  15 us
    ppermute x9, starting transfers between devices, ring(): return lax.ppermute(value, axis, [((i + shift) % 4, i) for i in range(4)])  13.4 us
  transfers between devices with their start and end apart: 32, of which 19 were waited for; matrix products, arithmetic and copies ran while one was open for 6% of the time, Pallas kernels for 12%

profile of v2, /device:TPU:1, one launch (start us, length us, event | category | flops | bytes accessed | tf_op | source)
XLA Modules:
  0.0 246.4 jit_solution(16060979207308544639)
XLA Ops:
  18.9 3.3 %collective-permute-done.2 = f32[2,16,1024]{2,1,0:T(8,128)S(1)} collective-permute-done((f32[2,16,1024]{2,1,0:T(8,128)S(1)}, f32[2,16,1024]{2,1,0:T(8,128)S(1)}, u32[]{:S(2)}, u32[]{:S(2)}) %collective-permute-start.2) | collective-permute-done | bytes 131104 | tf_op jit(solution)/shard_map/ppermute | solution.py:22
  27.1 8.2 %shard_map.95.refs_3_ = f32[256,2048]{1,0:T(8,128)} custom-call(f32[128,1024]{1,0:T(8,128)} %bitcast.74, f32[128,1024]{1,0:T(8,128)} %copy-done.20, bf16[256,256]{1,0:T(8,128)(2,1)} %fusion.2.refs_2_, f32[1024,2048]{1,0:T(8,128)} %refs_7_.3, f32[8,2048]{1,0:T(8,128)} %broadcast_bitcast_fusion.refs_4_.refs_8_), custom_call_target="tpu_custom_call" | custom-call | flops 3221225472 | bytes 11534336 | tf_op jit(solution)/shard_map/pallas_call | solution.py:108
  42.0 2.9 %collective-permute-done.8.refs_2_ = f32[64,1024]{1,0:T(8,128)S(1)} collective-permute-done((f32[64,1024]{1,0:T(8,128)S(1)}, f32[64,1024]{1,0:T(8,128)S(1)}, u32[]{:S(2)}, u32[]{:S(2)}) %collective-permute-start.8) | collective-permute-done | bytes 262176 | tf_op jit(solution)/shard_map/ppermute | solution.py:22
  45.0 6.7 %collective-permute-done.7.refs_1_ = f32[64,1024]{1,0:T(8,128)S(1)} collective-permute-done((f32[64,1024]{1,0:T(8,128)S(1)}, f32[64,1024]{1,0:T(8,128)S(1)}, u32[]{:S(2)}, u32[]{:S(2)}) %collective-permute-start.7) | collective-permute-done | bytes 262176 | tf_op jit(solution)/shard_map/ppermute | solution.py:22
  57.5 10.2 %shard_map.97 = (f32[192,2048]{1,0:T(8,128)}, f32[48,2048]{1,0:T(8,128)}, f32[48,2048]{1,0:T(8,128)}, f32[48,2048]{1,0:T(8,128)}, f32[48,2048]{1,0:T(8,128)}) custom-call(f32[64,1024]{1,0:T(8,128)} %get-tuple-element.18.refs_0_.refs_1_, f32[64,1024]{1,0:T(8,128)} %get-tuple-element.19.refs_1_.refs_2_, f32[64,1024]{1,0:T(8,128)} %get-tuple-element.20.refs_2_.refs_3_, ...), custom_call_target="tpu_custom_call" | custom-call | flops 4831838208 | bytes 13107200 | tf_op jit(solution)/shard_map/pallas_call | solution.py:108
  67.7 5.2 %collective-permute-start.14 = (f32[48,2048]{1,0:T(8,128)}, f32[48,2048]{1,0:T(8,128)S(1)}, u32[]{:S(2)}, u32[]{:S(2)}) collective-permute-start(f32[48,2048]{1,0:T(8,128)} %get-tuple-element.25), channel_id=1, source_target_pairs={{0,3},{128,131},{1,0},{129,128},{2,1},{130,129},{3,2},{131,130},{4... | collective-permute-start | bytes 1179656 | tf_op jit(solution)/shard_map/ppermute | solution.py:18
  77.3 4.7 %collective-permute-done.18.refs_2_ = f32[64,1024]{1,0:T(8,128)S(1)} collective-permute-done((f32[64,1024]{1,0:T(8,128)}, f32[64,1024]{1,0:T(8,128)S(1)}, u32[]{:S(2)}, u32[]{:S(2)}) %collective-permute-start.18) | collective-permute-done | bytes 262176 | tf_op jit(solution)/shard_map/ppermute | solution.py:22
  82.0 4.9 %collective-permute-done.17.refs_1_ = f32[64,1024]{1,0:T(8,128)S(1)} collective-permute-done((f32[64,1024]{1,0:T(8,128)}, f32[64,1024]{1,0:T(8,128)S(1)}, u32[]{:S(2)}, u32[]{:S(2)}) %collective-permute-start.17) | collective-permute-done | bytes 262176 | tf_op jit(solution)/shard_map/ppermute | solution.py:22
  90.7 7.4 %collective-permute-done.14 = f32[48,2048]{1,0:T(8,128)S(1)} collective-permute-done((f32[48,2048]{1,0:T(8,128)}, f32[48,2048]{1,0:T(8,128)S(1)}, u32[]{:S(2)}, u32[]{:S(2)}) %collective-permute-start.14) | collective-permute-done | bytes 393248 | tf_op jit(solution)/shard_map/ppermute | solution.py:18
  98.2 6.5 %collective-permute-start.15 = (f32[48,2048]{1,0:T(8,128)S(1)}, f32[48,2048]{1,0:T(8,128)S(1)}, u32[]{:S(2)}, u32[]{:S(2)}) collective-permute-start(f32[48,2048]{1,0:T(8,128)S(1)} %add.259), channel_id=1, source_target_pairs={{0,131},{128,0},{1,128},{129,1},{2,129},{130,2},{3,130},{131,3},{4... | collective-permute-start | bytes 1179656 | tf_op jit(solution)/shard_map/ppermute | solution.py:18
  108.2 4.6 %collective-permute-done.15.refs_10_ = f32[48,2048]{1,0:T(8,128)S(1)} collective-permute-done((f32[48,2048]{1,0:T(8,128)S(1)}, f32[48,2048]{1,0:T(8,128)S(1)}, u32[]{:S(2)}, u32[]{:S(2)}) %collective-permute-start.15) | collective-permute-done | bytes 393248 | tf_op jit(solution)/shard_map/ppermute | solution.py:18
  112.8 3.2 %collective-permute-done.13.refs_9_ = f32[48,2048]{1,0:T(8,128)S(1)} collective-permute-done((f32[48,2048]{1,0:T(8,128)S(1)}, f32[48,2048]{1,0:T(8,128)S(1)}, u32[]{:S(2)}, u32[]{:S(2)}) %collective-permute-start.13) | collective-permute-done | bytes 393248 | tf_op jit(solution)/shard_map/ppermute | solution.py:18
  116.0 3.7 %collective-permute-done.5.refs_11_ = f32[32,2048]{1,0:T(8,128)S(1)} collective-permute-done((f32[32,2048]{1,0:T(8,128)S(1)}, f32[32,2048]{1,0:T(8,128)S(1)}, u32[]{:S(2)}, u32[]{:S(2)}) %collective-permute-start.5) | collective-permute-done | bytes 262176 | tf_op jit(solution)/shard_map/ppermute | solution.py:215
  120.4 10.1 %shard_map.101 = (f32[96,2048]{1,0:T(8,128)}, f32[96,2048]{1,0:T(8,128)}, f32[72,2048]{1,0:T(8,128)}, f32[72,2048]{1,0:T(8,128)}, f32[48,2048]{1,0:T(8,128)}) custom-call(f32[64,1024]{1,0:T(8,128)} %get-tuple-element.26.refs_0_, f32[64,1024]{1,0:T(8,128)} %get-tuple-element.27.refs_1_, f32[64,1024]{1,0:T(8,128)} %get-tuple-element.28.refs_2_, ...), custom_call_target="tpu_custom_call" | custom-call | flops 4831838208 | bytes 13107200 | tf_op jit(solution)/shard_map/pallas_call | solution.py:108
  134.8 36.4 %reduce-scatter.5.cloned.1.call-done = f32[48,2048]{1,0:T(8,128)} async-done(((f32[192,2048]{1,0:T(8,128)}), f32[48,2048]{1,0:T(8,128)}) %reduce-scatter.5.cloned.1.call-update) | async-done | bytes 393232 | tf_op jit(solution)/shard_map/reduce_scatter | solution.py:196
  171.2 4.7 %shard_map.98 = f32[32,64,128]{2,1,0:T(8,128)} custom-call(s32[2]{0:T(128)} %pad_add_fusion.place_ref, f32[4,8,2048]{2,1,0:T(8,128)} %get-tuple-element.39.own_n, f32[4,8,2048]{2,1,0:T(8,128)} %bitcast.70, f32[2,3,8,2048]{3,2,1,0:T(8,128)} %bitcast.75, f32[2,3,8,2048]{3,2,1,0:T(8,128)} %bitcast.77, f32[2,3,8,2048]{3,2,1,0:T(8,128)} %bitcast.76), custom_call_target="tpu_custom_call" | custom-call | bytes 1048576 | tf_op jit(solution)/shard_map/pallas_call | solution.py:56
  175.9 8.5 %all-to-all-start = ((f32[32,64,128]{2,1,0:T(8,128)}), f32[32,64,128]{2,1,0:T(8,128)S(1)}, u32[]{:S(2)}, u32[]{:S(2)}) async-start(f32[32,64,128]{2,1,0:T(8,128)} %shard_map.98), calls=%async_computation.2 | async-start | bytes 2097152 | tf_op jit(solution)/shard_map/all_to_all | solution.py:210
  186.1 3.2 %collective-permute-start.24 = (f32[24,2048]{1,0:T(8,128)S(1)}, f32[24,2048]{1,0:T(8,128)S(1)}, u32[]{:S(2)}, u32[]{:S(2)}) collective-permute-start(f32[24,2048]{1,0:T(8,128)S(1)} %slice.62), channel_id=1, source_target_pairs={{0,3},{128,131},{1,0},{129,128},{2,1},{130,129},{3,2},{131,130},{4... | collective-permute-start | bytes 589832 | tf_op jit(solution)/shard_map/ppermute | solution.py:18
  189.5 2.7 %collective-permute-start.27 = (f32[48,2048]{1,0:T(8,128)S(1)}, f32[48,2048]{1,0:T(8,128)S(1)}, u32[]{:S(2)}, u32[]{:S(2)}) collective-permute-start(f32[48,2048]{1,0:T(8,128)S(1)} %slice.67), channel_id=1, source_target_pairs={{0,131},{128,0},{1,128},{129,1},{2,129},{130,2},{3,130},{131,3},{4... | collective-permute-start | bytes 1179656 | tf_op jit(solution)/shard_map/ppermute | solution.py:18
  196.1 6.6 %collective-permute-done.26 = f32[48,2048]{1,0:T(8,128)S(1)} collective-permute-done((f32[48,2048]{1,0:T(8,128)S(1)}, f32[48,2048]{1,0:T(8,128)S(1)}, u32[]{:S(2)}, u32[]{:S(2)}) %collective-permute-start.26) | collective-permute-done | bytes 393248 | tf_op jit(solution)/shard_map/ppermute | solution.py:18
  204.9 4.8 %shard_map.102 = f32[32,64,128]{2,1,0:T(8,128)} custom-call(s32[2]{0:T(128)} %pad_add_fusion.place_ref, f32[4,8,2048]{2,1,0:T(8,128)} %get-tuple-element.39.own_n, f32[4,8,2048]{2,1,0:T(8,128)} %bitcast.71, f32[2,3,8,2048]{3,2,1,0:T(8,128)} %bitcast.69, f32[2,3,8,2048]{3,2,1,0:T(8,128)} %bitcast.78, f32[2,3,8,2048]{3,2,1,0:T(8,128)} %bitcast.79), custom_call_target="tpu_custom_call" | custom-call | bytes 1048576 | tf_op jit(solution)/shard_map/pallas_call | solution.py:56
  209.7 7.3 %all-to-all-start.1 = ((f32[32,64,128]{2,1,0:T(8,128)}), f32[32,64,128]{2,1,0:T(8,128)S(1)}, u32[]{:S(2)}, u32[]{:S(2)}) async-start(f32[32,64,128]{2,1,0:T(8,128)} %shard_map.102), calls=%async_computation.3 | async-start | bytes 2097152 | tf_op jit(solution)/shard_map/all_to_all | solution.py:210
  219.3 15.0 %all-to-all-done.1 = f32[32,64,128]{2,1,0:T(8,128)S(1)} async-done(((f32[32,64,128]{2,1,0:T(8,128)}), f32[32,64,128]{2,1,0:T(8,128)S(1)}, u32[]{:S(2)}, u32[]{:S(2)}) %all-to-all-start.1) | async-done | bytes 1048608 | tf_op jit(solution)/shard_map/all_to_all | solution.py:210
  236.2 3.3 %subtract_divide_fusion = (f32[4,131072]{1,0:T(4,128)}, f32[4,131072]{1,0:T(4,128)}) fusion(f32[4]{0:T(128)S(1)} %select_reduce_fusion.1, f32[131072]{0:T(1024)S(1)} %copy-done.6, f32[2,131072]{1,0:T(2,128)S(1)} %bitcast.68, f32[2,131072]{1,0:T(2,128)S(1)} %bitcast.67), kind=kLoop, calls=%fused_computation.1 | loop fusion | flops 1572864 | bytes 6815760 | tf_op jit(solution)/shard_map/div | solution.py:256
  (178 shorter events, 57.7 us)
Async XLA Ops:
  7.2 97.7 %reduce-scatter.3.cloned.1.call-start = ((), (), s32[]{:S(2)}) async-start(), calls=%async_computation.4 | async-start | bytes 2621440 | tf_op jit(solution)/shard_map/reduce_scatter | solution.py:196
  35.3 135.9 %reduce-scatter.5.cloned.1.call-start = ((), (), s32[]{:S(2)}) async-start(), calls=%async_computation.5 | async-start | bytes 1966080 | tf_op jit(solution)/shard_map/reduce_scatter | solution.py:196
  36.3 8.7 %collective-permute-start.8 = (f32[64,1024]{1,0:T(8,128)S(1)}, f32[64,1024]{1,0:T(8,128)S(1)}, u32[]{:S(2)}, u32[]{:S(2)}) collective-permute-start(f32[64,1024]{1,0:T(8,128)S(1)} %bitcast.82), channel_id=1, source_target_pairs={{96,0},{0,32},{32,64},{64,96},{97,1},{1,33},{33,65},{65,97},{98,2}... | collective-permute-start | bytes 786440 | tf_op jit(solution)/shard_map/ppermute | solution.py:22
  37.4 14.3 %collective-permute-start.7 = (f32[64,1024]{1,0:T(8,128)S(1)}, f32[64,1024]{1,0:T(8,128)S(1)}, u32[]{:S(2)}, u32[]{:S(2)}) collective-permute-start(f32[64,1024]{1,0:T(8,128)S(1)} %bitcast.83), channel_id=1, source_target_pairs={{64,0},{96,32},{0,64},{32,96},{65,1},{97,33},{1,65},{33,97},{66,2}... | collective-permute-start | bytes 786440 | tf_op jit(solution)/shard_map/ppermute | solution.py:22
  40.0 11.7 %collective-permute-start.6 = (f32[64,1024]{1,0:T(8,128)S(1)}, f32[64,1024]{1,0:T(8,128)S(1)}, u32[]{:S(2)}, u32[]{:S(2)}) collective-permute-start(f32[64,1024]{1,0:T(8,128)S(1)} %bitcast.84), channel_id=1, source_target_pairs={{32,0},{64,32},{96,64},{0,96},{33,1},{65,33},{97,65},{1,97},{34,2}... | collective-permute-start | bytes 786440 | tf_op jit(solution)/shard_map/ppermute | solution.py:22
  67.7 30.4 %collective-permute-start.14 = (f32[48,2048]{1,0:T(8,128)}, f32[48,2048]{1,0:T(8,128)S(1)}, u32[]{:S(2)}, u32[]{:S(2)}) collective-permute-start(f32[48,2048]{1,0:T(8,128)} %get-tuple-element.25), channel_id=1, source_target_pairs={{0,3},{128,131},{1,0},{129,128},{2,1},{130,129},{3,2},{131,130},{4... | collective-permute-start | bytes 1179656 | tf_op jit(solution)/shard_map/ppermute | solution.py:18
  72.9 31.8 %collective-permute-start.12 = (f32[48,2048]{1,0:T(8,128)}, f32[48,2048]{1,0:T(8,128)S(1)}, u32[]{:S(2)}, u32[]{:S(2)}) collective-permute-start(f32[48,2048]{1,0:T(8,128)} %get-tuple-element.23.refs_3_), channel_id=1, source_target_pairs={{0,1},{128,129},{1,2},{129,130},{2,3},{130,131},{3,0},{131,128},{4... | collective-permute-start | bytes 1179656 | tf_op jit(solution)/shard_map/ppermute | solution.py:18
  72.9 9.1 %collective-permute-start.18 = (f32[64,1024]{1,0:T(8,128)}, f32[64,1024]{1,0:T(8,128)S(1)}, u32[]{:S(2)}, u32[]{:S(2)}) collective-permute-start(f32[64,1024]{1,0:T(8,128)} %shard_map.99), channel_id=1, source_target_pairs={{96,0},{0,32},{32,64},{64,96},{97,1},{1,33},{33,65},{65,97},{98,2}... | collective-permute-start | bytes 786440 | tf_op jit(solution)/shard_map/ppermute | solution.py:22
  73.0 13.8 %collective-permute-start.17 = (f32[64,1024]{1,0:T(8,128)}, f32[64,1024]{1,0:T(8,128)S(1)}, u32[]{:S(2)}, u32[]{:S(2)}) collective-permute-start(f32[64,1024]{1,0:T(8,128)} %shard_map.99), channel_id=1, source_target_pairs={{64,0},{96,32},{0,64},{32,96},{65,1},{97,33},{1,65},{33,97},{66,2}... | collective-permute-start | bytes 786440 | tf_op jit(solution)/shard_map/ppermute | solution.py:22
  75.2 12.6 %collective-permute-start.16 = (f32[64,1024]{1,0:T(8,128)}, f32[64,1024]{1,0:T(8,128)S(1)}, u32[]{:S(2)}, u32[]{:S(2)}) collective-permute-start(f32[64,1024]{1,0:T(8,128)} %shard_map.99), channel_id=1, source_target_pairs={{32,0},{64,32},{96,64},{0,96},{33,1},{65,33},{97,65},{1,97},{34,2}... | collective-permute-start | bytes 786440 | tf_op jit(solution)/shard_map/ppermute | solution.py:22
  88.5 18.1 %collective-permute-start.19 = (f32[64,1024]{1,0:T(8,128)}, f32[64,1024]{1,0:T(8,128)S(1)}, u32[]{:S(2)}, u32[]{:S(2)}) collective-permute-start(f32[64,1024]{1,0:T(8,128)} %get-tuple-element.26.refs_0_), channel_id=1, source_target_pairs={{0,4},{4,0},{1,5},{5,1},{2,6},{6,2},{3,7},{7,3},{8,12},{12,8},{9,1... | collective-permute-start | bytes 786440 | tf_op jit(solution)/shard_map/ppermute | solution.py:149
  90.2 18.0 %collective-permute-start.20 = (f32[64,1024]{1,0:T(8,128)}, f32[64,1024]{1,0:T(8,128)S(1)}, u32[]{:S(2)}, u32[]{:S(2)}) collective-permute-start(f32[64,1024]{1,0:T(8,128)} %get-tuple-element.27.refs_1_), channel_id=1, source_target_pairs={{0,4},{4,0},{1,5},{5,1},{2,6},{6,2},{3,7},{7,3},{8,12},{12,8},{9,1... | collective-permute-start | bytes 786440 | tf_op jit(solution)/shard_map/ppermute | solution.py:149
  90.2 18.0 %collective-permute-start.21 = (f32[64,1024]{1,0:T(8,128)}, f32[64,1024]{1,0:T(8,128)S(1)}, u32[]{:S(2)}, u32[]{:S(2)}) collective-permute-start(f32[64,1024]{1,0:T(8,128)} %get-tuple-element.28.refs_2_), channel_id=1, source_target_pairs={{0,4},{4,0},{1,5},{5,1},{2,6},{6,2},{3,7},{7,3},{8,12},{12,8},{9,1... | collective-permute-start | bytes 786440 | tf_op jit(solution)/shard_map/ppermute | solution.py:149
  98.2 14.6 %collective-permute-start.15 = (f32[48,2048]{1,0:T(8,128)S(1)}, f32[48,2048]{1,0:T(8,128)S(1)}, u32[]{:S(2)}, u32[]{:S(2)}) collective-permute-start(f32[48,2048]{1,0:T(8,128)S(1)} %add.259), channel_id=1, source_target_pairs={{0,131},{128,0},{1,128},{129,1},{2,129},{130,2},{3,130},{131,3},{4... | collective-permute-start | bytes 1179656 | tf_op jit(solution)/shard_map/ppermute | solution.py:18
  104.7 11.3 %collective-permute-start.13 = (f32[48,2048]{1,0:T(8,128)S(1)}, f32[48,2048]{1,0:T(8,128)S(1)}, u32[]{:S(2)}, u32[]{:S(2)}) collective-permute-start(f32[48,2048]{1,0:T(8,128)S(1)} %add.258), channel_id=1, source_target_pairs={{0,128},{128,1},{1,129},{129,2},{2,130},{130,3},{3,131},{131,0},{4... | collective-permute-start | bytes 1179656 | tf_op jit(solution)/shard_map/ppermute | solution.py:18
  106.6 13.1 %collective-permute-start.5 = (f32[32,2048]{1,0:T(8,128)S(1)}, f32[32,2048]{1,0:T(8,128)S(1)}, u32[]{:S(2)}, u32[]{:S(2)}) collective-permute-start(f32[32,2048]{1,0:T(8,128)S(1)} %get-tuple-element.38), channel_id=1, source_target_pairs={{0,128},{128,0},{1,129},{129,1},{2,130},{130,2},{3,131},{131,3},{4... | collective-permute-start | bytes 786440 | tf_op jit(solution)/shard_map/ppermute | solution.py:215
  130.5 53.9 %collective-permute-start.22 = (f32[96,2048]{1,0:T(8,128)}, f32[96,2048]{1,0:T(8,128)S(1)}, u32[]{:S(2)}, u32[]{:S(2)}) collective-permute-start(f32[96,2048]{1,0:T(8,128)} %get-tuple-element.30), channel_id=1, source_target_pairs={{0,1},{128,129},{1,2},{129,130},{2,3},{130,131},{3,0},{131,128},{4... | collective-permute-start | bytes 2359304 | tf_op jit(solution)/shard_map/ppermute | solution.py:18
  131.6 54.4 %collective-permute-start.23 = (f32[96,2048]{1,0:T(8,128)}, f32[96,2048]{1,0:T(8,128)S(1)}, u32[]{:S(2)}, u32[]{:S(2)}) collective-permute-start(f32[96,2048]{1,0:T(8,128)} %get-tuple-element.32), channel_id=1, source_target_pairs={{0,3},{128,131},{1,0},{129,128},{2,1},{130,129},{3,2},{131,130},{4... | collective-permute-start | bytes 2359304 | tf_op jit(solution)/shard_map/ppermute | solution.py:18
  175.9 33.8 %all-to-all-start = ((f32[32,64,128]{2,1,0:T(8,128)}), f32[32,64,128]{2,1,0:T(8,128)S(1)}, u32[]{:S(2)}, u32[]{:S(2)}) async-start(f32[32,64,128]{2,1,0:T(8,128)} %shard_map.98), calls=%async_computation.2 | async-start | bytes 2097152 | tf_op jit(solution)/shard_map/all_to_all | solution.py:210
  185.6 8.5 %collective-permute-start.25 = (f32[24,2048]{1,0:T(8,128)S(1)}, f32[24,2048]{1,0:T(8,128)S(1)}, u32[]{:S(2)}, u32[]{:S(2)}) collective-permute-start(f32[24,2048]{1,0:T(8,128)S(1)} %slice.65), channel_id=1, source_target_pairs={{0,1},{128,129},{1,2},{129,130},{2,3},{130,131},{3,0},{131,128},{4... | collective-permute-start | bytes 589832 | tf_op jit(solution)/shard_map/ppermute | solution.py:18
  186.1 9.1 %collective-permute-start.24 = (f32[24,2048]{1,0:T(8,128)S(1)}, f32[24,2048]{1,0:T(8,128)S(1)}, u32[]{:S(2)}, u32[]{:S(2)}) collective-permute-start(f32[24,2048]{1,0:T(8,128)S(1)} %slice.62), channel_id=1, source_target_pairs={{0,3},{128,131},{1,0},{129,128},{2,1},{130,129},{3,2},{131,130},{4... | collective-permute-start | bytes 589832 | tf_op jit(solution)/shard_map/ppermute | solution.py:18
  189.5 13.3 %collective-permute-start.26 = (f32[48,2048]{1,0:T(8,128)S(1)}, f32[48,2048]{1,0:T(8,128)S(1)}, u32[]{:S(2)}, u32[]{:S(2)}) collective-permute-start(f32[48,2048]{1,0:T(8,128)S(1)} %slice.66), channel_id=1, source_target_pairs={{0,128},{128,1},{1,129},{129,2},{2,130},{130,3},{3,131},{131,0},{4... | collective-permute-start | bytes 1179656 | tf_op jit(solution)/shard_map/ppermute | solution.py:18
  189.5 14.6 %collective-permute-start.27 = (f32[48,2048]{1,0:T(8,128)S(1)}, f32[48,2048]{1,0:T(8,128)S(1)}, u32[]{:S(2)}, u32[]{:S(2)}) collective-permute-start(f32[48,2048]{1,0:T(8,128)S(1)} %slice.67), channel_id=1, source_target_pairs={{0,131},{128,0},{1,128},{129,1},{2,129},{130,2},{3,130},{131,3},{4... | collective-permute-start | bytes 1179656 | tf_op jit(solution)/shard_map/ppermute | solution.py:18
  209.7 24.5 %all-to-all-start.1 = ((f32[32,64,128]{2,1,0:T(8,128)}), f32[32,64,128]{2,1,0:T(8,128)S(1)}, u32[]{:S(2)}, u32[]{:S(2)}) async-start(f32[32,64,128]{2,1,0:T(8,128)} %shard_map.102), calls=%async_computation.3 | async-start | bytes 2097152 | tf_op jit(solution)/shard_map/all_to_all | solution.py:210
  (35 other events, 231.5 us)
Sparse Core Ops, SparseCore 0:
  35.4 66.2 reduce-scatter.2
  105.1 66.1 reduce-scatter.4

commit v3 on v2

--- a/solution.py
+++ b/solution.py
@@ -140,9 +140,8 @@
     block_mask = jnp.sum(jnp.where(cd_hot & ab_hot, allowed[None, None], 0), axis=(2, 3)).astype(jnp.float32)
     mask_rows = jnp.repeat(block_mask, BLK, axis=1)
 
-    mine = amplitudes.reshape(4, 2, 2, depth).transpose(1, 0, 2, 3).reshape(2, 8, depth)
-    theirs = lax.ppermute(mine, "zl", [(0, 1), (1, 0)])
-    flat = jnp.concatenate([mine, theirs], axis=1)
+    theirs = lax.ppermute(amplitudes, "zl", [(0, 1), (1, 0)])
+    flat = jnp.concatenate([amplitudes, theirs], axis=0)
     in_x = jnp.stack([flat] + [ring("x", flat, shift) for shift in (1, 2, 3)], axis=0)
 
     def other_core(value):
@@ -159,7 +158,7 @@
         r, s, h, i, _, at_x, at_c = iotas(4, 2, 2, 2, 1, 4, 2)
         piece = jnp.where(at_c == c, 0, 1)
         dx = lax.rem(at_x - x + 4, 4)
-        return order_of(((((piece * 4 + dx) * 2 + h) * 2 + s) * 4 + r) * 2 + i, 256)
+        return order_of(((((piece * 4 + dx) * 2 + s) * 4 + r) * 2 + h) * 2 + i, 256)
 
     def far_order():
         o, i, dy, at_x, at_c = iotas(8, 2, 3, 4, 2)
@@ -218,20 +217,22 @@
     sizes = (192, 48, 48, 48, 48)
 
     def gathered(half, before, after):
-        pieces = in_x[:, half].reshape(64, depth)
+        pieces = in_x.reshape(4, 8, 2, 2, depth)[:, :, half].reshape(64, depth)
         if before:
             (pieces,) = gate([pieces], before)
-        pieces = list(gate([ring("y", pieces, shift) for shift in (1, 2, 3)], after))
+        pieces = [ring("y", pieces, shift) for shift in (1, 2, 3)]
+        if after:
+            pieces = list(gate(pieces, after))
         return pieces + [other_core(value) for value in pieces]
 
-    far_a = gathered(0, (), part_near)
-    part_a = product(far_a, order, sizes)
+    far_a = gathered(0, (), ())
+    part_a = product(far_a, order, sizes, *part_near)
     own_a = own_sum(part_a)
     first_a = first_stage(part_a)
 
     far_b = gathered(1, far_a[:3], part_a[1:2])
     second_a = second_stage(part_a, first_a)
-    part_b = product(far_b, last_order(), (96, 96, 72, 72, 48), *second_a, sums_near[1])
+    part_b = product(far_b, last_order(), (96, 96, 72, 72, 48), *second_a)
     first_b = first_stage((None, *part_b[:2]))
     sent_a = packed(0, sums_near, (own_a,) + second_a)
     out_a = to_owners(sent_a)

time: 247 us -> 265 us (1.073)
  waiting for transfers between devices: 106 us -> 126 us
  starting transfers between devices: 60.7 us -> 55.8 us
    ppermute x10, waiting for transfers between devices: 26.4 us -> 77.3 us  [z_shift(): lax.ppermute(value, Z, [(at[z], at[(z + shift) % 8]) for z in range(8)])]
    reduce_scatter x2, waiting for transfers between devices: 36.4 us -> 0.01 us  [own_sum(): return lax.psum_scatter(part[0], 'row', scatter_dimension=0, tiled=True)]
    ppermute x9, waiting for transfers between devices: 23.4 us -> 28.4 us  [ring(): return lax.ppermute(value, axis, [((i + shift) % 4, i) for i in range(4)])]
    unnamed x57 -> x59, local copies, waits for them, and re-layouts: 7.13 us -> 7.56 us
  transfers between devices with their start and end apart: 32 -> 32, of which waited for: 19 -> 19; matrix products, arithmetic and copies ran while one was open for 6% -> 7% of each run, Pallas kernels for 12% -> 11%
where the time goes in v3:
time: 265 us; the launch traced here: 264 us
  waiting for transfers between devices  126 us (48%)
  starting transfers between devices  55.8 us (21%)
  Pallas kernels  38.2 us (14%)
  local copies, waits for them, and re-layouts  17.2 us (6%)
  between operations  14.6 us (6%)
  other arithmetic  11.5 us (4%)
    ppermute x10, waiting for transfers between devices, z_shift(): lax.ppermute(value, Z, [(at[z], at[(z + shift) % 8]) for z in range(8)])  77.3 us
    pallas_call x3, Pallas kernels, multiply(): pl.pallas_call(kernel, grid=(cols // tile,), in_specs=[pl.BlockSpec(piece...  28.8 us
    ppermute x9, waiting for transfers between devices, ring(): return lax.ppermute(value, axis, [((i + shift) % 4, i) for i in range(4)])  28.4 us
    ppermute x10, starting transfers between devices, z_shift(): lax.ppermute(value, Z, [(at[z], at[(z + shift) % 8]) for z in range(8)])  21.2 us
    all_to_all x2, waiting for transfers between devices, to_owners(): return lax.all_to_all(sent, PLANE, 0, 0, tiled=True)  15 us
    all_to_all x2, starting transfers between devices, to_owners(): return lax.all_to_all(sent, PLANE, 0, 0, tiled=True)  14.6 us
    ppermute x9, starting transfers between devices, ring(): return lax.ppermute(value, axis, [((i + shift) % 4, i) for i in range(4)])  12.5 us
    pallas_call x2, Pallas kernels, pack(): pl.pallas_call(kernel, grid_spec=pltpu.PrefetchScalarGridSpec(num_scalar_...  9.43 us
  transfers between devices with their start and end apart: 32, of which 19 were waited for; matrix products, arithmetic and copies ran while one was open for 7% of the time, Pallas kernels for 11%

profile of v3, /device:TPU:1, one launch (start us, length us, event | category | flops | bytes accessed | tf_op | source)
XLA Modules:
  0.0 263.8 jit_solution(13149751151744246143)
XLA Ops:
  21.1 3.8 %collective-permute-done.3 = f32[32,1024]{1,0:T(8,128)S(1)} collective-permute-done((f32[32,1024]{1,0:T(8,128)S(1)}, f32[32,1024]{1,0:T(8,128)S(1)}, u32[]{:S(2)}, u32[]{:S(2)}) %collective-permute-start.3) | collective-permute-done | bytes 131104 | tf_op jit(solution)/shard_map/ppermute | solution.py:22
  28.4 8.2 %shard_map.95.refs_9_ = f32[256,2048]{1,0:T(8,128)} custom-call(f32[128,1024]{1,0:T(8,128)} %bitcast.73, f32[128,1024]{1,0:T(8,128)} %copy-done.19, bf16[256,256]{1,0:T(8,128)(2,1)} %fusion.2.refs_2_, f32[1024,2048]{1,0:T(8,128)} %refs_7_.3, f32[8,2048]{1,0:T(8,128)} %broadcast_bitcast_fusion.refs_4_.refs_8_), custom_call_target="tpu_custom_call" | custom-call | flops 3221225472 | bytes 11534336 | tf_op jit(solution)/shard_map/pallas_call | solution.py:108
  37.7 3.0 %collective-permute-start.7 = (f32[64,1024]{1,0:T(8,128)S(1)}, f32[64,1024]{1,0:T(8,128)S(1)}, u32[]{:S(2)}, u32[]{:S(2)}) collective-permute-start(f32[64,1024]{1,0:T(8,128)S(1)} %reshape_squeeze.6), channel_id=1, source_target_pairs={{64,0},{96,32},{0,64},{32,96},{65,1},{97,33},{1,65},{33,97},{66,2}... | collective-permute-start | bytes 786440 | tf_op jit(solution)/shard_map/ppermute | solution.py:22
  48.9 4.4 %collective-permute-done.8.refs_2_.refs_3_ = f32[64,1024]{1,0:T(8,128)S(1)} collective-permute-done((f32[64,1024]{1,0:T(8,128)S(1)}, f32[64,1024]{1,0:T(8,128)S(1)}, u32[]{:S(2)}, u32[]{:S(2)}) %collective-permute-start.8) | collective-permute-done | bytes 262176 | tf_op jit(solution)/shard_map/ppermute | solution.py:22
  56.4 10.2 %shard_map.96 = (f32[192,2048]{1,0:T(8,128)}, f32[48,2048]{1,0:T(8,128)}, f32[48,2048]{1,0:T(8,128)}, f32[48,2048]{1,0:T(8,128)}, f32[48,2048]{1,0:T(8,128)}) custom-call(f32[64,1024]{1,0:T(8,128)} %copy-done.12, f32[64,1024]{1,0:T(8,128)} %copy-done.10, f32[64,1024]{1,0:T(8,128)} %copy-done.11, f32[64,1024]{1,0:T(8,128)} %copy-done.25, ...), custom_call_target="tpu_custom_call" | custom-call | flops 4831838208 | bytes 13107200 | tf_op jit(solution)/shard_map/pallas_call | solution.py:108
  66.6 5.2 %collective-permute-start.14 = (f32[48,2048]{1,0:T(8,128)}, f32[48,2048]{1,0:T(8,128)S(1)}, u32[]{:S(2)}, u32[]{:S(2)}) collective-permute-start(f32[48,2048]{1,0:T(8,128)} %get-tuple-element.19), channel_id=1, source_target_pairs={{0,3},{128,131},{1,0},{129,128},{2,1},{130,129},{3,2},{131,130},{4... | collective-permute-start | bytes 1179656 | tf_op jit(solution)/shard_map/ppermute | solution.py:18
  76.6 4.8 %collective-permute-done.16.refs_0_ = f32[64,1024]{1,0:T(8,128)S(1)} collective-permute-done((f32[64,1024]{1,0:T(8,128)}, f32[64,1024]{1,0:T(8,128)S(1)}, u32[]{:S(2)}, u32[]{:S(2)}) %collective-permute-start.16) | collective-permute-done | bytes 262176 | tf_op jit(solution)/shard_map/ppermute | solution.py:22
  84.0 6.7 %collective-permute-done.18.refs_2_ = f32[64,1024]{1,0:T(8,128)S(1)} collective-permute-done((f32[64,1024]{1,0:T(8,128)}, f32[64,1024]{1,0:T(8,128)S(1)}, u32[]{:S(2)}, u32[]{:S(2)}) %collective-permute-start.18) | collective-permute-done | bytes 262176 | tf_op jit(solution)/shard_map/ppermute | solution.py:22
  92.3 5.5 %collective-permute-done.14 = f32[48,2048]{1,0:T(8,128)S(1)} collective-permute-done((f32[48,2048]{1,0:T(8,128)}, f32[48,2048]{1,0:T(8,128)S(1)}, u32[]{:S(2)}, u32[]{:S(2)}) %collective-permute-start.14) | collective-permute-done | bytes 393248 | tf_op jit(solution)/shard_map/ppermute | solution.py:18
  97.9 6.4 %collective-permute-start.15 = (f32[48,2048]{1,0:T(8,128)S(1)}, f32[48,2048]{1,0:T(8,128)S(1)}, u32[]{:S(2)}, u32[]{:S(2)}) collective-permute-start(f32[48,2048]{1,0:T(8,128)S(1)} %add.259), channel_id=1, source_target_pairs={{0,131},{128,0},{1,128},{129,1},{2,129},{130,2},{3,130},{131,3},{4... | collective-permute-start | bytes 1179656 | tf_op jit(solution)/shard_map/ppermute | solution.py:18
  105.3 7.0 %collective-permute-done.15.refs_10_ = f32[48,2048]{1,0:T(8,128)S(1)} collective-permute-done((f32[48,2048]{1,0:T(8,128)S(1)}, f32[48,2048]{1,0:T(8,128)S(1)}, u32[]{:S(2)}, u32[]{:S(2)}) %collective-permute-start.15) | collective-permute-done | bytes 393248 | tf_op jit(solution)/shard_map/ppermute | solution.py:18
  112.3 3.2 %collective-permute-done.13.refs_9_ = f32[48,2048]{1,0:T(8,128)S(1)} collective-permute-done((f32[48,2048]{1,0:T(8,128)S(1)}, f32[48,2048]{1,0:T(8,128)S(1)}, u32[]{:S(2)}, u32[]{:S(2)}) %collective-permute-start.13) | collective-permute-done | bytes 393248 | tf_op jit(solution)/shard_map/ppermute | solution.py:18
  116.3 10.4 %shard_map.100 = (f32[96,2048]{1,0:T(8,128)}, f32[96,2048]{1,0:T(8,128)}, f32[72,2048]{1,0:T(8,128)}, f32[72,2048]{1,0:T(8,128)}, f32[48,2048]{1,0:T(8,128)}) custom-call(f32[64,1024]{1,0:T(8,128)} %get-tuple-element.20.refs_0_, f32[64,1024]{1,0:T(8,128)} %get-tuple-element.21.refs_1_, f32[64,1024]{1,0:T(8,128)} %get-tuple-element.22.refs_2_, ...), custom_call_target="tpu_custom_call" | custom-call | flops 4831838208 | bytes 13107200 | tf_op jit(solution)/shard_map/pallas_call | solution.py:108
  127.6 3.6 %collective-permute-start.23 = (f32[96,2048]{1,0:T(8,128)}, f32[96,2048]{1,0:T(8,128)S(1)}, u32[]{:S(2)}, u32[]{:S(2)}) collective-permute-start(f32[96,2048]{1,0:T(8,128)} %get-tuple-element.26), channel_id=1, source_target_pairs={{0,3},{128,131},{1,0},{129,128},{2,1},{130,129},{3,2},{131,130},{4... | collective-permute-start | bytes 2359304 | tf_op jit(solution)/shard_map/ppermute | solution.py:18
  132.9 47.5 %collective-permute-done.22 = f32[96,2048]{1,0:T(8,128)S(1)} collective-permute-done((f32[96,2048]{1,0:T(8,128)}, f32[96,2048]{1,0:T(8,128)S(1)}, u32[]{:S(2)}, u32[]{:S(2)}) %collective-permute-start.22) | collective-permute-done | bytes 786464 | tf_op jit(solution)/shard_map/ppermute | solution.py:18
  182.4 4.8 %collective-permute-done.5 = f32[32,2048]{1,0:T(8,128)S(1)} collective-permute-done((f32[32,2048]{1,0:T(8,128)S(1)}, f32[32,2048]{1,0:T(8,128)S(1)}, u32[]{:S(2)}, u32[]{:S(2)}) %collective-permute-start.5) | collective-permute-done | bytes 262176 | tf_op jit(solution)/shard_map/ppermute | solution.py:214
  187.9 4.7 %shard_map.97 = f32[32,64,128]{2,1,0:T(8,128)} custom-call(s32[2]{0:T(128)} %pad_add_fusion.place_ref, f32[4,8,2048]{2,1,0:T(8,128)} %get-tuple-element.33.own_n, f32[4,8,2048]{2,1,0:T(8,128)} %bitcast.69, f32[2,3,8,2048]{3,2,1,0:T(8,128)} %bitcast.77, f32[2,3,8,2048]{3,2,1,0:T(8,128)} %bitcast.79, f32[2,3,8,2048]{3,2,1,0:T(8,128)} %bitcast.78), custom_call_target="tpu_custom_call" | custom-call | bytes 1048576 | tf_op jit(solution)/shard_map/pallas_call | solution.py:56
  192.6 7.3 %all-to-all-start = ((f32[32,64,128]{2,1,0:T(8,128)}), f32[32,64,128]{2,1,0:T(8,128)S(1)}, u32[]{:S(2)}, u32[]{:S(2)}) async-start(f32[32,64,128]{2,1,0:T(8,128)} %shard_map.97), calls=%async_computation.2 | async-start | bytes 2097152 | tf_op jit(solution)/shard_map/all_to_all | solution.py:209
  209.3 6.3 %collective-permute-done.26 = f32[48,2048]{1,0:T(8,128)S(1)} collective-permute-done((f32[48,2048]{1,0:T(8,128)S(1)}, f32[48,2048]{1,0:T(8,128)S(1)}, u32[]{:S(2)}, u32[]{:S(2)}) %collective-permute-start.26) | collective-permute-done | bytes 393248 | tf_op jit(solution)/shard_map/ppermute | solution.py:18
  215.6 6.0 %collective-permute-done.27 = f32[48,2048]{1,0:T(8,128)S(1)} collective-permute-done((f32[48,2048]{1,0:T(8,128)S(1)}, f32[48,2048]{1,0:T(8,128)S(1)}, u32[]{:S(2)}, u32[]{:S(2)}) %collective-permute-start.27) | collective-permute-done | bytes 393248 | tf_op jit(solution)/shard_map/ppermute | solution.py:18
  222.4 4.8 %shard_map.101 = f32[32,64,128]{2,1,0:T(8,128)} custom-call(s32[2]{0:T(128)} %pad_add_fusion.place_ref, f32[4,8,2048]{2,1,0:T(8,128)} %get-tuple-element.33.own_n, f32[4,8,2048]{2,1,0:T(8,128)} %bitcast.70, f32[2,3,8,2048]{3,2,1,0:T(8,128)} %bitcast.68, f32[2,3,8,2048]{3,2,1,0:T(8,128)} %bitcast.80, f32[2,3,8,2048]{3,2,1,0:T(8,128)} %bitcast.81), custom_call_target="tpu_custom_call" | custom-call | bytes 1048576 | tf_op jit(solution)/shard_map/pallas_call | solution.py:56
  227.2 7.3 %all-to-all-start.1 = ((f32[32,64,128]{2,1,0:T(8,128)}), f32[32,64,128]{2,1,0:T(8,128)S(1)}, u32[]{:S(2)}, u32[]{:S(2)}) async-start(f32[32,64,128]{2,1,0:T(8,128)} %shard_map.101), calls=%async_computation.3 | async-start | bytes 2097152 | tf_op jit(solution)/shard_map/all_to_all | solution.py:209
  236.7 15.0 %all-to-all-done.1 = f32[32,64,128]{2,1,0:T(8,128)S(1)} async-done(((f32[32,64,128]{2,1,0:T(8,128)}), f32[32,64,128]{2,1,0:T(8,128)S(1)}, u32[]{:S(2)}, u32[]{:S(2)}) %all-to-all-start.1) | async-done | bytes 1048608 | tf_op jit(solution)/shard_map/all_to_all | solution.py:209
  253.6 3.3 %subtract_divide_fusion = (f32[4,131072]{1,0:T(4,128)}, f32[4,131072]{1,0:T(4,128)}) fusion(f32[4]{0:T(128)S(1)} %select_reduce_fusion.1, f32[131072]{0:T(1024)S(1)} %copy-done.2, f32[2,131072]{1,0:T(2,128)S(1)} %bitcast.67, f32[2,131072]{1,0:T(2,128)S(1)} %bitcast.66), kind=kLoop, calls=%fused_computation.1 | loop fusion | flops 1572864 | bytes 6815760 | tf_op jit(solution)/shard_map/div | solution.py:257
  (181 shorter events, 60.1 us)
Async XLA Ops:
  7.2 123.9 %reduce-scatter.3.cloned.1.call-start = ((), (), s32[]{:S(2)}) async-start(), calls=%async_computation.4 | async-start | bytes 2621440 | tf_op jit(solution)/shard_map/reduce_scatter | solution.py:195
  16.2 8.7 %collective-permute-start.3 = (f32[32,1024]{1,0:T(8,128)S(1)}, f32[32,1024]{1,0:T(8,128)S(1)}, u32[]{:S(2)}, u32[]{:S(2)}) collective-permute-start(f32[32,1024]{1,0:T(8,128)S(1)} %constant_dynamic-update-slice_fusion), channel_id=1, source_target_pairs={{24,0},{0,8},{8,16},{16,24},{25,1},{1,9},{9,17},{17,25},{26,2},{2,... | collective-permute-start | bytes 393224 | tf_op jit(solution)/shard_map/ppermute | solution.py:22
  36.6 145.8 %reduce-scatter.5.cloned.1.call-start = ((), (), s32[]{:S(2)}) async-start(), calls=%async_computation.5 | async-start | bytes 1966080 | tf_op jit(solution)/shard_map/reduce_scatter | solution.py:195
  37.7 9.1 %collective-permute-start.7 = (f32[64,1024]{1,0:T(8,128)S(1)}, f32[64,1024]{1,0:T(8,128)S(1)}, u32[]{:S(2)}, u32[]{:S(2)}) collective-permute-start(f32[64,1024]{1,0:T(8,128)S(1)} %reshape_squeeze.6), channel_id=1, source_target_pairs={{64,0},{96,32},{0,64},{32,96},{65,1},{97,33},{1,65},{33,97},{66,2}... | collective-permute-start | bytes 786440 | tf_op jit(solution)/shard_map/ppermute | solution.py:22
  40.7 12.5 %collective-permute-start.8 = (f32[64,1024]{1,0:T(8,128)S(1)}, f32[64,1024]{1,0:T(8,128)S(1)}, u32[]{:S(2)}, u32[]{:S(2)}) collective-permute-start(f32[64,1024]{1,0:T(8,128)S(1)} %reshape_squeeze.6), channel_id=1, source_target_pairs={{96,0},{0,32},{32,64},{64,96},{97,1},{1,33},{33,65},{65,97},{98,2}... | collective-permute-start | bytes 786440 | tf_op jit(solution)/shard_map/ppermute | solution.py:22
  41.1 12.5 %collective-permute-start.6 = (f32[64,1024]{1,0:T(8,128)S(1)}, f32[64,1024]{1,0:T(8,128)S(1)}, u32[]{:S(2)}, u32[]{:S(2)}) collective-permute-start(f32[64,1024]{1,0:T(8,128)S(1)} %reshape_squeeze.6), channel_id=1, source_target_pairs={{32,0},{64,32},{96,64},{0,96},{33,1},{65,33},{97,65},{1,97},{34,2}... | collective-permute-start | bytes 786440 | tf_op jit(solution)/shard_map/ppermute | solution.py:22
  66.6 31.2 %collective-permute-start.14 = (f32[48,2048]{1,0:T(8,128)}, f32[48,2048]{1,0:T(8,128)S(1)}, u32[]{:S(2)}, u32[]{:S(2)}) collective-permute-start(f32[48,2048]{1,0:T(8,128)} %get-tuple-element.19), channel_id=1, source_target_pairs={{0,3},{128,131},{1,0},{129,128},{2,1},{130,129},{3,2},{131,130},{4... | collective-permute-start | bytes 1179656 | tf_op jit(solution)/shard_map/ppermute | solution.py:18
  71.8 32.5 %collective-permute-start.12 = (f32[48,2048]{1,0:T(8,128)}, f32[48,2048]{1,0:T(8,128)S(1)}, u32[]{:S(2)}, u32[]{:S(2)}) collective-permute-start(f32[48,2048]{1,0:T(8,128)} %get-tuple-element.17.refs_3_), channel_id=1, source_target_pairs={{0,1},{128,129},{1,2},{129,130},{2,3},{130,131},{3,0},{131,128},{4... | collective-permute-start | bytes 1179656 | tf_op jit(solution)/shard_map/ppermute | solution.py:18
  72.7 8.7 %collective-permute-start.16 = (f32[64,1024]{1,0:T(8,128)}, f32[64,1024]{1,0:T(8,128)S(1)}, u32[]{:S(2)}, u32[]{:S(2)}) collective-permute-start(f32[64,1024]{1,0:T(8,128)} %shard_map.98), channel_id=1, source_target_pairs={{32,0},{64,32},{96,64},{0,96},{33,1},{65,33},{97,65},{1,97},{34,2}... | collective-permute-start | bytes 786440 | tf_op jit(solution)/shard_map/ppermute | solution.py:22
  75.0 9.0 %collective-permute-start.17 = (f32[64,1024]{1,0:T(8,128)}, f32[64,1024]{1,0:T(8,128)S(1)}, u32[]{:S(2)}, u32[]{:S(2)}) collective-permute-start(f32[64,1024]{1,0:T(8,128)} %shard_map.98), channel_id=1, source_target_pairs={{64,0},{96,32},{0,64},{32,96},{65,1},{97,33},{1,65},{33,97},{66,2}... | collective-permute-start | bytes 786440 | tf_op jit(solution)/shard_map/ppermute | solution.py:22
  75.8 14.9 %collective-permute-start.18 = (f32[64,1024]{1,0:T(8,128)}, f32[64,1024]{1,0:T(8,128)S(1)}, u32[]{:S(2)}, u32[]{:S(2)}) collective-permute-start(f32[64,1024]{1,0:T(8,128)} %shard_map.98), channel_id=1, source_target_pairs={{96,0},{0,32},{32,64},{64,96},{97,1},{1,33},{33,65},{65,97},{98,2}... | collective-permute-start | bytes 786440 | tf_op jit(solution)/shard_map/ppermute | solution.py:22
  91.4 13.8 %collective-permute-start.19 = (f32[64,1024]{1,0:T(8,128)}, f32[64,1024]{1,0:T(8,128)S(1)}, u32[]{:S(2)}, u32[]{:S(2)}) collective-permute-start(f32[64,1024]{1,0:T(8,128)} %get-tuple-element.20.refs_0_), channel_id=1, source_target_pairs={{0,4},{4,0},{1,5},{5,1},{2,6},{6,2},{3,7},{7,3},{8,12},{12,8},{9,1... | collective-permute-start | bytes 786440 | tf_op jit(solution)/shard_map/ppermute | solution.py:148
  91.8 13.4 %collective-permute-start.20 = (f32[64,1024]{1,0:T(8,128)}, f32[64,1024]{1,0:T(8,128)S(1)}, u32[]{:S(2)}, u32[]{:S(2)}) collective-permute-start(f32[64,1024]{1,0:T(8,128)} %get-tuple-element.21.refs_1_), channel_id=1, source_target_pairs={{0,4},{4,0},{1,5},{5,1},{2,6},{6,2},{3,7},{7,3},{8,12},{12,8},{9,1... | collective-permute-start | bytes 786440 | tf_op jit(solution)/shard_map/ppermute | solution.py:148
  91.9 13.3 %collective-permute-start.21 = (f32[64,1024]{1,0:T(8,128)}, f32[64,1024]{1,0:T(8,128)S(1)}, u32[]{:S(2)}, u32[]{:S(2)}) collective-permute-start(f32[64,1024]{1,0:T(8,128)} %get-tuple-element.22.refs_2_), channel_id=1, source_target_pairs={{0,4},{4,0},{1,5},{5,1},{2,6},{6,2},{3,7},{7,3},{8,12},{12,8},{9,1... | collective-permute-start | bytes 786440 | tf_op jit(solution)/shard_map/ppermute | solution.py:148
  97.9 14.4 %collective-permute-start.15 = (f32[48,2048]{1,0:T(8,128)S(1)}, f32[48,2048]{1,0:T(8,128)S(1)}, u32[]{:S(2)}, u32[]{:S(2)}) collective-permute-start(f32[48,2048]{1,0:T(8,128)S(1)} %add.259), channel_id=1, source_target_pairs={{0,131},{128,0},{1,128},{129,1},{2,129},{130,2},{3,130},{131,3},{4... | collective-permute-start | bytes 1179656 | tf_op jit(solution)/shard_map/ppermute | solution.py:18
  104.3 11.2 %collective-permute-start.13 = (f32[48,2048]{1,0:T(8,128)S(1)}, f32[48,2048]{1,0:T(8,128)S(1)}, u32[]{:S(2)}, u32[]{:S(2)}) collective-permute-start(f32[48,2048]{1,0:T(8,128)S(1)} %add.258), channel_id=1, source_target_pairs={{0,128},{128,1},{1,129},{129,2},{2,130},{130,3},{3,131},{131,0},{4... | collective-permute-start | bytes 1179656 | tf_op jit(solution)/shard_map/ppermute | solution.py:18
  126.7 53.7 %collective-permute-start.22 = (f32[96,2048]{1,0:T(8,128)}, f32[96,2048]{1,0:T(8,128)S(1)}, u32[]{:S(2)}, u32[]{:S(2)}) collective-permute-start(f32[96,2048]{1,0:T(8,128)} %get-tuple-element.24), channel_id=1, source_target_pairs={{0,1},{128,129},{1,2},{129,130},{2,3},{130,131},{3,0},{131,128},{4... | collective-permute-start | bytes 2359304 | tf_op jit(solution)/shard_map/ppermute | solution.py:18
  127.6 72.3 %collective-permute-start.23 = (f32[96,2048]{1,0:T(8,128)}, f32[96,2048]{1,0:T(8,128)S(1)}, u32[]{:S(2)}, u32[]{:S(2)}) collective-permute-start(f32[96,2048]{1,0:T(8,128)} %get-tuple-element.26), channel_id=1, source_target_pairs={{0,3},{128,131},{1,0},{129,128},{2,1},{130,129},{3,2},{131,130},{4... | collective-permute-start | bytes 2359304 | tf_op jit(solution)/shard_map/ppermute | solution.py:18
  132.9 54.3 %collective-permute-start.5 = (f32[32,2048]{1,0:T(8,128)S(1)}, f32[32,2048]{1,0:T(8,128)S(1)}, u32[]{:S(2)}, u32[]{:S(2)}) collective-permute-start(f32[32,2048]{1,0:T(8,128)S(1)} %get-tuple-element.32), channel_id=1, source_target_pairs={{0,128},{128,0},{1,129},{129,1},{2,130},{130,2},{3,131},{131,3},{4... | collective-permute-start | bytes 786440 | tf_op jit(solution)/shard_map/ppermute | solution.py:214
  182.2 24.5 %collective-permute-start.25 = (f32[24,2048]{1,0:T(8,128)}, f32[24,2048]{1,0:T(8,128)S(1)}, u32[]{:S(2)}, u32[]{:S(2)}) collective-permute-start(f32[24,2048]{1,0:T(8,128)} %slice.65), channel_id=1, source_target_pairs={{0,1},{128,129},{1,2},{129,130},{2,3},{130,131},{3,0},{131,128},{4... | collective-permute-start | bytes 589832 | tf_op jit(solution)/shard_map/ppermute | solution.py:18
  192.6 34.6 %all-to-all-start = ((f32[32,64,128]{2,1,0:T(8,128)}), f32[32,64,128]{2,1,0:T(8,128)S(1)}, u32[]{:S(2)}, u32[]{:S(2)}) async-start(f32[32,64,128]{2,1,0:T(8,128)} %shard_map.97), calls=%async_computation.2 | async-start | bytes 2097152 | tf_op jit(solution)/shard_map/all_to_all | solution.py:209
  203.6 12.0 %collective-permute-start.26 = (f32[48,2048]{1,0:T(8,128)S(1)}, f32[48,2048]{1,0:T(8,128)S(1)}, u32[]{:S(2)}, u32[]{:S(2)}) collective-permute-start(f32[48,2048]{1,0:T(8,128)S(1)} %slice.66), channel_id=1, source_target_pairs={{0,128},{128,1},{1,129},{129,2},{2,130},{130,3},{3,131},{131,0},{4... | collective-permute-start | bytes 1179656 | tf_op jit(solution)/shard_map/ppermute | solution.py:18
  205.8 15.8 %collective-permute-start.27 = (f32[48,2048]{1,0:T(8,128)S(1)}, f32[48,2048]{1,0:T(8,128)S(1)}, u32[]{:S(2)}, u32[]{:S(2)}) collective-permute-start(f32[48,2048]{1,0:T(8,128)S(1)} %slice.67), channel_id=1, source_target_pairs={{0,131},{128,0},{1,128},{129,1},{2,129},{130,2},{3,130},{131,3},{4... | collective-permute-start | bytes 1179656 | tf_op jit(solution)/shard_map/ppermute | solution.py:18
  227.2 24.5 %all-to-all-start.1 = ((f32[32,64,128]{2,1,0:T(8,128)}), f32[32,64,128]{2,1,0:T(8,128)S(1)}, u32[]{:S(2)}, u32[]{:S(2)}) async-start(f32[32,64,128]{2,1,0:T(8,128)} %shard_map.101), calls=%async_computation.3 | async-start | bytes 2097152 | tf_op jit(solution)/shard_map/all_to_all | solution.py:209
  (34 other events, 230.3 us)
Sparse Core Ops, SparseCore 0:
  36.8 64.8 reduce-scatter.2
  104.9 66.5 reduce-scatter.4
